TPU v7x, 512 devices: a whole 4x8x8 slice. The times are simulated.
512 devices in a mesh: space: 64 (over y, z), chan: 8 (over x, core).
Axes of the slice: x: 4, y: 8, z: 8, core: 2. Of those that a mesh axis runs over, the one named last changes fastest.
Arguments:
- state_field: bfloat16 [384, 192, 1440], P('chan', 'space'), may hold values from -6 to 6
- slot_wave: int32 [1152], replicated, may hold values from 0 to 720, as said below
- spectral_filter: bfloat16 [1152, 2, 384, 720], P('space', None, 'chan'), may hold values from -4 to 4
- kan_coef: bfloat16 [6, 384, 384], P(None, 'chan'), may hold values from -0.125 to 0.125
Outputs:
- mixed_out: bfloat16 [384, 192, 1440], P('chan', 'space')
Inputs may be any that keep to these rules, and one draw needn't show every extreme that they name: `slot_wave`: each wavenumber 0 to 719 is held by exactly one slot, every other slot holds 720; owner d holds slots d * 18 to (d+1) * 18 - 1, and some owner has all its slots filled.
All inputs are finite; a program needn't handle non-finite values.
Results may differ from a plain program's by a relative error of at most 0.025.
Values may be sent and summed in bfloat16 or wider, within the bound.
A program may use at most 128 MiB of HBM per device.

v0:
```python
import math

import jax
import jax.numpy as jnp
from jax import lax
from jax.sharding import PartitionSpec as P

NLON = 1440
MMAX = 720
LMAX = 720
BASIS = 6


def zonal_tables(nlon, wave_total):
    wave_order = jnp.arange(wave_total, dtype=jnp.int32)
    points = jnp.arange(nlon, dtype=jnp.int32)
    phases = wave_order[:, None] * points[None, :] % nlon
    angles = phases.astype(jnp.float32) * (2.0 * math.pi / nlon)
    cosine = jnp.cos(angles)
    sine_part = jnp.sin(angles)
    forward = jnp.stack([cosine, -sine_part], axis=1).reshape(2 * wave_total, nlon) / nlon
    factor = jnp.where(wave_order == 0, 1.0, 2.0).astype(jnp.float32)[:, None]
    inverse = jnp.stack([factor * cosine, -factor * sine_part], axis=1).reshape(
        2 * wave_total, nlon
    )
    return (forward.astype(jnp.bfloat16), inverse.astype(jnp.bfloat16))


def band_grid(lat_all, lmax):
    row_index = jnp.arange(lat_all, dtype=jnp.int32).astype(jnp.float32)
    colatitude = 0.5 * math.pi + (row_index + 0.5 - 0.5 * lat_all) * (math.pi / lmax)
    weights = 2.0 * math.pi * math.pi / lmax * jnp.sin(colatitude)
    return (colatitude, weights)


def legendre_table(wave_ids, colatitude, lmax):
    cosine = jnp.cos(colatitude)[None, :]
    wave_order = wave_ids.astype(jnp.float32)[:, None]
    log_first = 0.5 * (
        jnp.log((2.0 * wave_order + 1.0) / (4.0 * math.pi))
        + lax.lgamma(wave_order + 0.5)
        - lax.lgamma(wave_order + 1.0)
        - 0.5 * math.log(math.pi)
    )
    first_value = jnp.exp(log_first + wave_order * jnp.log(jnp.sin(colatitude))[None, :])
    per_block = 1
    for candidate in (24, 20, 16, 12, 10, 8, 6, 4, 2):
        if lmax % candidate == 0 and per_block == 1:
            per_block = candidate

    def advance(state_pair, block_index):
        before, earlier = state_pair
        collected = []
        for offset in range(per_block):
            degree = (block_index * per_block + offset).astype(jnp.float32)
            prior_degree = degree - 1.0
            rising = jnp.sqrt(
                (4.0 * degree * degree - 1.0)
                / jnp.maximum(degree * degree - wave_order * wave_order, 1.0)
            )
            falling = jnp.sqrt(
                jnp.maximum(prior_degree * prior_degree - wave_order * wave_order, 0.0)
                / (4.0 * prior_degree * prior_degree - 1.0)
            )
            general = rising * (cosine * before - falling * earlier)
            second = cosine * jnp.sqrt(2.0 * wave_order + 3.0) * before
            current = jnp.where(
                degree < wave_order,
                0.0,
                jnp.where(
                    degree == wave_order,
                    first_value,
                    jnp.where(degree == wave_order + 1.0, second, general),
                ),
            )
            earlier = before
            before = current
            collected.append(current)
        return ((before, earlier), jnp.stack(collected))

    zero_state = jnp.zeros((wave_ids.shape[0], colatitude.shape[0]), jnp.float32)
    _, stacked = lax.scan(
        advance, (zero_state, zero_state), jnp.arange(lmax // per_block, dtype=jnp.int32)
    )
    return stacked.reshape(lmax, wave_ids.shape[0], colatitude.shape[0])


def filter_modes(spectrum, filter_gain):
    count = spectrum.shape[0]
    shaped = spectrum.reshape(count, 2, filter_gain.shape[2], filter_gain.shape[3])
    real_part = shaped[:, 0]
    imag_part = shaped[:, 1]
    gain_real = filter_gain[:, 0]
    gain_imag = filter_gain[:, 1]
    result = jnp.stack(
        [
            gain_real * real_part - gain_imag * imag_part,
            gain_real * imag_part + gain_imag * real_part,
        ],
        axis=1,
    )
    return result.reshape(spectrum.shape).astype(jnp.bfloat16)


def expand_basis(activity):
    upcast = activity.astype(jnp.float32)
    squashed = jnp.tanh(upcast)
    constant = jnp.ones_like(squashed)
    quadratic = 2.0 * squashed * squashed - 1.0
    cubic_term = 2.0 * squashed * quadratic - squashed
    quartic = 2.0 * squashed * cubic_term - quadratic
    base_branch = upcast * jax.nn.sigmoid(upcast)
    return jnp.stack([base_branch, constant, squashed, quadratic, cubic_term, quartic]).astype(
        jnp.bfloat16
    )


def shards(state_field, slot_wave, spectral_filter, kan_coef):
    chan_dev = state_field.shape[0]
    lat_dev = state_field.shape[1]
    spaces = lax.axis_size("space")
    lat_all = lat_dev * spaces
    slot_count = spectral_filter.shape[0]
    row_count = lat_dev * NLON
    forward, inverse = zonal_tables(NLON, MMAX)
    zonal_coeff = lax.dot_general(
        forward, state_field, (((1,), (2,)), ((), ())), preferred_element_type=jnp.float32
    )
    zonal_coeff = zonal_coeff.astype(jnp.bfloat16).reshape(MMAX, 2, chan_dev, lat_dev)
    padded = jnp.concatenate(
        [zonal_coeff, jnp.zeros((1, 2, chan_dev, lat_dev), jnp.bfloat16)], axis=0
    )
    packed = jnp.take(padded, slot_wave, axis=0).reshape(spaces, slot_count, 2, chan_dev, lat_dev)
    arrived = lax.all_to_all(packed, "space", split_axis=0, concat_axis=4, tiled=True)
    arrived = arrived.reshape(slot_count, 2 * chan_dev, lat_all)
    owned_waves = lax.dynamic_slice_in_dim(
        slot_wave, lax.axis_index("space") * slot_count, slot_count
    )
    colatitude, weights = band_grid(lat_all, LMAX)
    legendre = legendre_table(owned_waves, colatitude, LMAX)
    analysis = (legendre * weights[None, None, :]).astype(jnp.bfloat16)
    synthesis = legendre.astype(jnp.bfloat16)
    spectrum = lax.dot_general(
        arrived, analysis, (((2,), (2,)), ((0,), (1,))), preferred_element_type=jnp.float32
    )
    filtered = filter_modes(spectrum, spectral_filter.astype(jnp.float32))
    rebuilt = lax.dot_general(
        filtered, synthesis, (((2,), (0,)), ((0,), (1,))), preferred_element_type=jnp.float32
    )
    rebuilt = rebuilt.astype(jnp.bfloat16).reshape(1, slot_count, 2, chan_dev, lat_all)
    returned = lax.all_to_all(rebuilt, "space", split_axis=4, concat_axis=0, tiled=True)
    returned = returned.reshape(spaces * slot_count, 2, chan_dev, lat_dev)
    matches = (slot_wave[None, :] == jnp.arange(MMAX, dtype=jnp.int32)[:, None]).astype(jnp.int32)
    position = jnp.sum(matches * jnp.arange(spaces * slot_count, dtype=jnp.int32)[None, :], axis=1)
    unpacked = jnp.take(returned, position, axis=0).reshape(2 * MMAX, chan_dev, lat_dev)
    spatial = lax.dot_general(
        unpacked, inverse, (((0,), (0,)), ((), ())), preferred_element_type=jnp.float32
    )
    updated = (state_field.astype(jnp.float32) + spatial).astype(jnp.bfloat16)
    basis_rows = expand_basis(updated.reshape(chan_dev, row_count)).reshape(
        BASIS * chan_dev, row_count
    )
    flat_coef = kan_coef.reshape(BASIS * chan_dev, kan_coef.shape[2])
    summed = lax.psum_scatter(
        lax.dot_general(
            flat_coef, basis_rows, (((0,), (0,)), ((), ())), preferred_element_type=jnp.float32
        ).astype(jnp.bfloat16),
        "chan",
        scatter_dimension=0,
        tiled=True,
    )
    return summed.reshape(chan_dev, lat_dev, NLON)


def solution(mesh):
    in_specs = (
        P("chan", "space", None),
        P(),
        P("space", None, "chan", None),
        P(None, "chan", None),
    )
    out_specs = P("chan", "space", None)
    return jax.shard_map(shards, mesh=mesh, in_specs=in_specs, out_specs=out_specs, check_vma=False)
```

profile of v0, /device:TPU:8, one launch (start us, length us, event | category | flops | bytes accessed | tf_op | source)
XLA Modules:
  0.0 409.4 jit_solution(1990531605449050881)
XLA Ops:
  6.5 18.6 %fusion.93 = (f32[720,1,1440]{2,0,1:T(8,128)S(1)}, f32[720,1,1440]{2,0,1:T(8,128)S(1)}) fusion(), kind=kLoop, calls=%fused_computation.275 | loop fusion | flops 10368000 | bytes 8294400 | tf_op jit(solution)/shard_map/cos | solution.py:19
  25.2 3.3 fusion.78
  28.5 8.9 %copy.35 = bf16[720,2,1440]{2,1,0:T(2,128)(2,1)} copy(bf16[720,2,1440]{2,0,1:T(8,128)(2,1)} %fusion.78) | data formatting | bytes 8294400 | tf_op jit(solution)/shard_map/convert_element_type | solution.py:26
  37.4 10.0 %reshape.2044 = bf16[1440,1440,1]{1,0,2:T(8,128)(2,1)} reshape(bf16[720,2,1440]{2,1,0:T(2,128)(2,1)} %copy.35) | data formatting | bytes 8294400 | tf_op jit(solution)/shard_map/convert_element_type | solution.py:26
  47.3 3.8 convolution_convert_fusion
  52.6 1.1 concatenate.3
  53.7 7.3 %gather_fusion = bf16[1152,2,48,3]{2,1,3,0:T(2,128)(2,1)S(1)} fusion(bf16[721,2,48,3]{2,1,3,0:T(2,128)(2,1)S(1)} %concatenate.3, s32[2048]{0:T(1024)S(1)} %pad_clamp_fusion), kind=kCustom, calls=%fused_computation | custom fusion | bytes 1331712 | tf_op jit(solution)/shard_map/jit(_take)/gather | solution.py:133
  61.1 4.1 fusion.151
  65.1 6.0 %reshape.2052 = bf16[64,2,2592]{2,1,0:T(2,128)(2,1)} reshape(bf16[64,18,3,2,48]{4,3,2,1,0:T(2,128)(2,1)} %fusion.151) | data formatting | bytes 1327104
  71.1 25.2 %all-to-all-start = ((bf16[64,2,2592]{2,1,0:T(2,128)(2,1)}), bf16[64,2,2592]{2,1,0:T(2,128)(2,1)S(1)}, u32[]{:S(2)}, u32[]{:S(2)}) async-start(bf16[64,2,2592]{2,1,0:T(2,128)(2,1)} %reshape.2052), calls=%async_computation | async-start | bytes 1376256 | tf_op jit(solution)/shard_map/all_to_all | solution.py:134
  96.5 153.8 %while.19 = (s32[]{:T(128)}, f32[18,192]{1,0:T(8,128)S(1)}, f32[18,192]{1,0:T(8,128)S(1)}, f32[30,24,18,192]{3,2,1,0:T(8,128)}, s32[30]{0:T(128)S(1)}, /*index=5...) while((s32[]{:T(128)}, f32[18,192]{1,0:T(8,128)S(1)}, ...), condition=%wide.region_2.3_spmd.clone.clone, body=%wide.region_1.2_spmd.clone.clone.sunk | while | flops 927746 | bytes 3413306 | solution.py:82
  105.9 0.9 bitcast_dynamic-update-slice_fusion.2
  141.7 0.9 bitcast_dynamic-update-slice_fusion.2
  152.0 0.9 bitcast_dynamic-update-slice_fusion.2
  162.2 0.9 bitcast_dynamic-update-slice_fusion.2
  167.4 0.9 bitcast_dynamic-update-slice_fusion.2
  172.5 0.9 bitcast_dynamic-update-slice_fusion.2
  182.8 0.9 bitcast_dynamic-update-slice_fusion.2
  203.3 0.9 bitcast_dynamic-update-slice_fusion.2
  208.4 0.9 bitcast_dynamic-update-slice_fusion.2
  213.6 0.9 bitcast_dynamic-update-slice_fusion.2
  228.9 0.9 bitcast_dynamic-update-slice_fusion.2
  234.1 0.9 bitcast_dynamic-update-slice_fusion.2
  249.4 0.9 bitcast_dynamic-update-slice_fusion.2
  250.3 15.6 %copy.39 = f32[720,18,192]{0,2,1:T(8,128)} copy(f32[720,18,192]{2,1,0:T(8,128)} %bitcast.501) | data formatting | bytes 19906560 | tf_op jit(solution)/shard_map/reshape | solution.py:85
  265.9 4.8 %convert_element_type.411 = f32[18,2,48,720]{3,2,1,0:T(8,128)} convert(bf16[18,2,48,720]{3,2,1,0:T(8,128)(2,1)} %param.8) | non-fusion elementwise | flops 1244160 | bytes 7464960 | tf_op jit(solution)/shard_map/convert_element_type | solution.py:146
  270.7 2.5 reshape.2053
  273.2 1.2 bitcast_bitcast_fusion
  274.5 1.7 copy.38
  276.2 1.6 reshape.2020
  277.8 8.2 %fusion.81 = f32[18,96,720]{2,1,0:T(8,128)} fusion(bf16[18,96,192]{1,2,0:T(8,128)(2,1)} %reshape.2020, f32[720,18,192]{0,2,1:T(8,128)} %copy.39, f32[192]{0:T(256)S(1)} %fusion.118), kind=kOutput, calls=%fused_computation.259 | convolution fusion | flops 482734080 | bytes 15594240 | tf_op jit(solution)/shard_map/dot_general | solution.py:143
  286.0 4.7 %subtract_convert_fusion = (bf16[18,1,48,720]{3,2,1,0:T(8,128)(2,1)S(1)}, bf16[18,1,48,720]{3,2,1,0:T(8,128)(2,1)S(1)}) fusion(f32[18,2,48,720]{3,2,1,0:T(8,128)} %bitcast.500, f32[18,2,48,720]{3,2,1,0:T(8,128)S(1)} %bitcast.499), kind=kLoop, calls=%fused_computation.283 | loop fusion | flops 4976640 | bytes 12441600 | tf_op jit(solution)/shard_map/convert.9
  291.0 1.8 fusion.100
  292.8 1.5 copy.42
  294.4 3.1 reshape.2054
  297.5 12.7 %all-to-all-start.1 = ((bf16[64,2,2592]{2,1,0:T(2,128)(2,1)}), bf16[64,2,2592]{2,1,0:T(2,128)(2,1)S(1)}, u32[]{:S(2)}, u32[]{:S(2)}) async-start(bf16[64,2,2592]{2,1,0:T(2,128)(2,1)} %reshape.2054), calls=%async_computation.1 | async-start | bytes 1376256 | tf_op jit(solution)/shard_map/all_to_all | solution.py:151
  310.7 20.2 %multiply_convert_fusion.2 = (bf16[720,1,1440]{2,0,1:T(8,128)(2,1)}, bf16[720,1,1440]{2,0,1:T(8,128)(2,1)}) fusion(f32[720]{0:T(1024)S(1)} %fusion.117, f32[720]{0:T(1024)S(1)} %fusion.115), kind=kLoop, calls=%fused_computation.269 | loop fusion | flops 13478400 | bytes 4152960 | tf_op jit(solution)/shard_map/convert.8
  331.2 2.5 reshape.2055
  333.7 1.7 copy.43
  335.4 1.2 copy.44
  336.7 4.5 %gather_fusion.1 = bf16[720,2,48,3]{2,1,3,0:T(2,128)(2,1)S(1)} fusion(bf16[1152,2,48,3]{2,1,3,0:T(2,128)(2,1)S(1)} %bitcast.495, s32[1024]{0:T(1024)S(1)} %pad_clamp_fusion.1), kind=kCustom, calls=%fused_computation.1 | custom fusion | bytes 832320 | tf_op jit(solution)/shard_map/jit(_take)/gather | solution.py:155
  341.2 3.0 broadcast_select_fusion.1
  344.2 3.2 fusion.99
  349.8 2.2 fusion.80
  352.1 5.2 %copy.50 = bf16[384,4320]{1,0:T(8,128)(2,1)} copy(bf16[384,4320]{0,1:T(8,128)(2,1)S(1)} %fusion.80) | data formatting | bytes 6635520
  357.3 42.1 %reduce-scatter.4.cloned.1.call-done = bf16[48,4320]{1,0:T(8,128)(2,1)} async-done(((bf16[384,4320]{1,0:T(8,128)(2,1)}), bf16[48,4320]{1,0:T(8,128)(2,1)}) %reduce-scatter.4.cloned.1.call-update) | async-done | bytes 414736
  399.4 1.5 copy.51
  401.0 1.2 copy.47
  (1090 shorter events, 116.1 us)
Async XLA Ops:
  6.5 343.3 %copy-start = (bf16[6,48,384]{2,1,0:T(8,128)(2,1)S(1)}, bf16[6,48,384]{2,1,0:T(8,128)(2,1)}, u32[]{:S(2)}) copy-start(bf16[6,48,384]{2,1,0:T(8,128)(2,1)} %param.9) | copy-start | bytes 663556
  6.5 18.6 %copy-start.1 = (s32[1152]{0:T(1024)S(1)}, s32[1152]{0:T(1024)}, u32[]{:S(2)}) copy-start(s32[1152]{0:T(1024)} %param.7) | copy-start | bytes 13828
  37.4 10.0 %copy-start.2 = (bf16[48,3,1440]{2,0,1:T(8,128)(2,1)S(1)}, bf16[48,3,1440]{2,0,1:T(8,128)(2,1)}, u32[]{:S(2)}) copy-start(bf16[48,3,1440]{2,0,1:T(8,128)(2,1)} %param.6) | copy-start | bytes 1244164
  71.1 199.6 %all-to-all-start = ((bf16[64,2,2592]{2,1,0:T(2,128)(2,1)}), bf16[64,2,2592]{2,1,0:T(2,128)(2,1)S(1)}, u32[]{:S(2)}, u32[]{:S(2)}) async-start(bf16[64,2,2592]{2,1,0:T(2,128)(2,1)} %reshape.2052), calls=%async_computation | async-start | bytes 1376256 | tf_op jit(solution)/shard_map/all_to_all | solution.py:134
  276.2 9.9 %slice-start.3 = ((s8[5308416]{0:T(1024)(128)(4,1)}), s8[1114112]{0:T(1024)(128)(4,1)S(1)}, s32[]{:S(2)}) async-start(s8[5308416]{0:T(1024)(128)(4,1)} %bitcast.498), calls=%async_computation.7 | async-start | bytes 2228224
  277.8 8.2 %slice-start.4 = ((s8[5308416]{0:T(1024)(128)(4,1)}), s8[4194304]{0:T(1024)(128)(4,1)S(1)}, s32[]{:S(2)}) async-start(s8[5308416]{0:T(1024)(128)(4,1)} %bitcast.498), calls=%async_computation.8 | async-start | bytes 8388608
  277.8 13.2 %slice-start = ((s8[10616832]{0:T(1024)(128)(4,1)}), s8[4194304]{0:T(1024)(128)(4,1)S(1)}, s32[]{:S(2)}) async-start(s8[10616832]{0:T(1024)(128)(4,1)} %bitcast.496), calls=%async_computation.4 | async-start | bytes 8388608
  277.8 13.2 %slice-start.1 = ((s8[10616832]{0:T(1024)(128)(4,1)}), s8[4194304]{0:T(1024)(128)(4,1)S(1)}, s32[]{:S(2)}) async-start(s8[10616832]{0:T(1024)(128)(4,1)} %bitcast.496), calls=%async_computation.5 | async-start | bytes 8388608
  286.0 5.0 %slice-start.2 = ((s8[10616832]{0:T(1024)(128)(4,1)}), s8[2228224]{0:T(1024)(128)(4,1)S(1)}, s32[]{:S(2)}) async-start(s8[10616832]{0:T(1024)(128)(4,1)} %bitcast.496), calls=%async_computation.6 | async-start | bytes 4456448
  297.5 33.7 %all-to-all-start.1 = ((bf16[64,2,2592]{2,1,0:T(2,128)(2,1)}), bf16[64,2,2592]{2,1,0:T(2,128)(2,1)S(1)}, u32[]{:S(2)}, u32[]{:S(2)}) async-start(bf16[64,2,2592]{2,1,0:T(2,128)(2,1)} %reshape.2054), calls=%async_computation.1 | async-start | bytes 1376256 | tf_op jit(solution)/shard_map/all_to_all | solution.py:151
  310.2 89.3 %reduce-scatter.4.cloned.1.call-start = ((), (), s32[]{:S(2)}) async-start(), calls=%async_computation.3 | async-start | bytes 3760128
  336.6 7.5 %copy-start.3 = (bf16[48,3,1440]{2,0,1:T(8,128)(2,1)S(1)}, bf16[48,3,1440]{2,0,1:T(8,128)(2,1)}, u32[]{:S(2)}) copy-start(bf16[48,3,1440]{2,0,1:T(8,128)(2,1)} %param.6) | copy-start | bytes 1244164
Sparse Core Ops, SparseCore 0:
  357.4 41.9 reduce-scatter.3
where the time goes:
time: 418 us; the launch traced here: 409 us
  other arithmetic  140 us (33%)
  local copies, waits for them, and re-layouts  124 us (30%)
  waiting for transfers between devices  42.4 us (10%)
  starting transfers between devices  37.9 us (9%)
  loops' own time  31.3 us (7%)
  matrix products  19.3 us (5%)
  between operations  14.2 us (3%)
    while x690, other arithmetic  66.5 us
    unnamed x2, waiting for transfers between devices  42.1 us
    another operation x1, loops' own time, legendre_table(): lax.scan(advance, (zero_state, zero_state), jnp.arange(lmax // per_block,...  31.3 us
    dynamic_update_slice x30, local copies, waits for them, and re-layouts, legendre_table(): lax.scan(advance, (zero_state, zero_state), jnp.arange(lmax // per_block,...  26.2 us
    all_to_all x1, starting transfers between devices, shards(): lax.all_to_all(packed, 'space', split_axis=0, concat_axis=4, tiled=True)  25.2 us
    another operation x2, other arithmetic  24.9 us
    unnamed x25, local copies, waits for them, and re-layouts  20.9 us
    convert_element_type x2, local copies, waits for them, and re-layouts, zonal_tables(): return (forward.astype(jnp.bfloat16), inverse.astype(jnp.bfloat16))  18.9 us
  transfers between devices with their start and end apart: 3, of which 2 were waited for; matrix products, arithmetic and copies ran while one was open for 40% of the time, Pallas kernels for 0%

commit v1 on v0

v1 whole, which is shorter than its diff:
```python
import math

import jax
import jax.numpy as jnp
import ml_dtypes
import numpy as np
from jax import lax
from jax.experimental import pallas as pl
from jax.experimental.pallas import tpu as pltpu
from jax.sharding import PartitionSpec as P

NLON = 1440
MMAX = 720
LMAX = 720
BASIS = 6
MPAD = 768
NPAD = 1536
SLOTS = 18
MAIN = 16
SPACES = 64
CHANS = 8
CDEV = 48
LDEV = 3
LAT = 192
ROWS = 48
COLS = 1408
PART = 640
DEG_SLOTS = 24
F32 = jnp.float32
BF16 = jnp.bfloat16

VMEM = pl.BlockSpec(memory_space=pltpu.VMEM)
SMEM = pl.BlockSpec(memory_space=pltpu.SMEM)
PARAMS = pltpu.CompilerParams(vmem_limit_bytes=56 * 1024 * 1024)


def make_tables():
    m = np.arange(MMAX)[:, None]
    n = np.arange(NLON)[None, :]
    angle = (m * n % NLON) * (2.0 * np.pi / NLON)
    cos, sin = np.cos(angle), np.sin(angle)
    forward = np.zeros((NLON, 2 * MPAD))
    forward[:, :MMAX] = cos.T / NLON
    forward[:, MPAD : MPAD + MMAX] = -sin.T / NLON
    factor = np.where(m == 0, 1.0, 2.0)
    inverse = np.zeros((2 * MPAD, NPAD))
    inverse[:MMAX, :NLON] = factor * cos
    inverse[MPAD : MPAD + MMAX, :NLON] = -factor * sin
    lat = np.arange(LAT)
    colat = 0.5 * np.pi + (lat + 0.5 - 0.5 * LAT) * (np.pi / LMAX)
    weights = (2.0 * np.pi * np.pi / LMAX * np.sin(colat)).astype(np.float32)
    order = (3 * np.arange(SPACES)[None, :] + np.arange(LDEV)[:, None]).reshape(-1)
    xrow = np.zeros((8, 256), np.float32)
    xrow[:, :LAT] = np.cos(colat)[order]
    first = np.zeros((MMAX + 8, 256), np.float32)
    for wave in range(MMAX):
        base = 0.5 * (
            math.log((2.0 * wave + 1.0) / (4.0 * math.pi))
            + math.lgamma(wave + 0.5)
            - math.lgamma(wave + 1.0)
            - 0.5 * math.log(math.pi)
        )
        first[wave, :LAT] = np.exp(base + wave * np.log(np.sin(colat)))[order]
    degree = np.arange(LMAX, dtype=np.float64)
    root = np.sqrt(np.maximum(4.0 * degree * degree - 1.0, 1.0))
    steps = np.stack([degree * degree, root, 1.0 / root]).astype(np.float32)
    return (
        forward.astype(ml_dtypes.bfloat16),
        inverse.astype(ml_dtypes.bfloat16),
        weights,
        xrow,
        first,
        steps,
    )


def one_hot(cols_row, start, size):
    waves = lax.broadcasted_iota(jnp.int32, (MPAD, size), 0)
    return jnp.where(waves == cols_row[0:1, start : start + size], 1.0, 0.0).astype(BF16)


def third_of(pair, shape):
    lane = lax.broadcasted_iota(jnp.int32, shape, 1)
    return jnp.where(lane >= 64, (2 * pair + 1) % 3, (2 * pair) % 3)


def pack_kernel(x_ref, table_ref, cols_ref, weight_ref, out_ref, zonal, packed, rows):
    here = lax.axis_index("space")
    for lat in range(LDEV):
        weight = weight_ref[here * LDEV + lat]
        for k in range(2):
            part = jnp.dot(
                x_ref[lat], table_ref[:, k * MPAD : (k + 1) * MPAD], preferred_element_type=F32
            )
            at = lat * 96 + k * CDEV
            zonal[at : at + CDEV, :] = (part * weight).astype(BF16)
    cols = cols_ref[...]
    coeff = zonal[...]
    for start in range(0, COLS, 128):
        packed[:, start : start + 128] = jnp.dot(
            coeff, one_hot(cols, start, 128), preferred_element_type=F32
        )
    for pair in range(MAIN // 2):
        for lat in range(LDEV):
            at = lat * 96
            main = packed[at : at + 96, pair * 128 : pair * 128 + 128]
            extra = jnp.zeros((32, 128), F32)
            if pair < 3:
                wide = packed[at : at + 96, 1024 + pair * 128 : 1024 + pair * 128 + 128]
                third = third_of(pair, (32, 128))
                for th in range(3):
                    extra = jnp.where(third == th, wide[th * 32 : th * 32 + 32], extra)
            turned = jnp.concatenate([main, extra], axis=0).T
            for half in range(2):
                at_row = lat * 16 + pair * 2 + half
                rows[pl.ds(at_row, 64, stride=ROWS), :] = turned[half * 64 : half * 64 + 64]
    out_ref[...] = rows[...].astype(BF16)


def legendre_kernel(wave_ref, steps_ref, x_ref, first_ref, out_ref, grown, order_ref, start_ref):
    base = lax.axis_index("space") * SLOTS
    for slot in range(DEG_SLOTS):
        wave = wave_ref[base + slot] if slot < SLOTS else MMAX
        order_ref[slot : slot + 1, :] = jnp.full((1, 128), wave, jnp.int32)
        start_ref[slot : slot + 1, :] = first_ref[pl.ds(wave, 1), :]
    order = order_ref[...]
    square = order.astype(F32) * order.astype(F32)
    first_a, first_b = start_ref[:, 0:128], start_ref[:, 128:256]
    x_a = jnp.broadcast_to(x_ref[0:1, 0:128], (DEG_SLOTS, 128))
    x_b = jnp.broadcast_to(x_ref[0:1, 128:256], (DEG_SLOTS, 128))

    def advance(block, carry):
        now_a, before_a, now_b, before_b, falling = carry
        for offset in range(8):
            degree = block * 8 + offset
            gap = steps_ref[0, degree] - square
            inverse_root = lax.rsqrt(jnp.maximum(gap, 1.0))
            rising = steps_ref[1, degree] * inverse_root
            starts = order == degree
            next_a = jnp.where(starts, first_a, rising * (x_a * now_a - falling * before_a))
            next_b = jnp.where(starts, first_b, rising * (x_b * now_b - falling * before_b))
            falling = gap * inverse_root * steps_ref[2, degree]
            now_a, before_a, now_b, before_b = next_a, now_a, next_b, now_b
            grown[0, pl.ds(degree * DEG_SLOTS, DEG_SLOTS), :] = next_a
            grown[1, pl.ds(degree * DEG_SLOTS, DEG_SLOTS), :] = next_b
        return now_a, before_a, now_b, before_b, falling

    zero = jnp.zeros((DEG_SLOTS, 128), F32)
    lax.fori_loop(0, LMAX // 8, advance, (zero, zero, zero, zero, zero))

    def spread(slot, carry):
        for half in range(2):
            out_ref[slot, :, half * 128 : half * 128 + 128] = grown[
                half, pl.ds(slot, LMAX, stride=DEG_SLOTS), :
            ].astype(BF16)
        return carry

    lax.fori_loop(0, SLOTS, spread, 0)


def spectral_kernel(rows_ref, table_ref, gain_ref, out_ref, rows, spread, made):
    rows[...] = rows_ref[...].astype(F32)
    for row in range(MAIN):
        stack = jnp.concatenate(
            [rows[pl.ds(lat * 16 + row, 64, stride=ROWS), :] for lat in range(LDEV)]
            + [jnp.zeros((64, 128), F32)],
            axis=0,
        )
        turned = stack.T.astype(BF16)
        spread[row] = turned[0:96]
        if row < 6:
            at = 32 * (row % 3)
            spread[MAIN + row // 3, at : at + 32, :] = turned[96:128]

    def one(slot, carry):
        table = table_ref[slot]
        spectrum = lax.dot_general(
            spread[slot], table, (((1,), (1,)), ((), ())), preferred_element_type=F32
        )
        real, imag = spectrum[0:CDEV], spectrum[CDEV:96]
        gain_real = gain_ref[slot, 0].astype(F32)
        gain_imag = gain_ref[slot, 1].astype(F32)
        filtered = jnp.concatenate(
            [gain_real * real - gain_imag * imag, gain_real * imag + gain_imag * real], axis=0
        ).astype(BF16)
        made[slot] = jnp.dot(filtered, table, preferred_element_type=F32)
        return carry

    lax.fori_loop(0, SLOTS, one, 0)
    for row in range(MAIN):
        extra = jnp.zeros((32, 256), F32)
        if row < 6:
            at = 32 * (row % 3)
            extra = made[MAIN + row // 3, at : at + 32, :]
        turned = jnp.concatenate([made[row], extra], axis=0).T
        for lat in range(LDEV):
            rows[pl.ds(lat * 16 + row, 64, stride=ROWS), :] = turned[lat * 64 : lat * 64 + 64]
    out_ref[...] = rows[...].astype(BF16)


def inverse_kernel(rows_ref, table_ref, cols_ref, x_ref, out_ref, rows, gathered, modes):
    rows[...] = rows_ref[...].astype(F32)
    for pair in range(MAIN // 2):
        for lat in range(LDEV):
            at = lat * 96
            turned = (
                jnp.concatenate(
                    [
                        rows[pl.ds(lat * 16 + pair * 2 + half, 64, stride=ROWS), :]
                        for half in range(2)
                    ],
                    axis=0,
                )
            ).T
            gathered[at : at + 96, pair * 128 : pair * 128 + 128] = turned[0:96].astype(BF16)
            if pair < 3:
                third = third_of(pair, (32, 128))
                for th in range(3):
                    gathered[
                        at + th * 32 : at + th * 32 + 32,
                        1024 + pair * 128 : 1024 + pair * 128 + 128,
                    ] = jnp.where(third == th, turned[96:128], 0.0).astype(BF16)
    cols = cols_ref[...]
    total = jnp.zeros((288, MPAD), F32)
    for start in range(0, COLS, 128):
        total += lax.dot_general(
            gathered[:, start : start + 128],
            one_hot(cols, start, 128),
            (((1,), (1,)), ((), ())),
            preferred_element_type=F32,
        )
    for lat in range(LDEV):
        for k in range(2):
            at = lat * 96 + k * CDEV
            modes[lat * CDEV : lat * CDEV + CDEV, k * MPAD : (k + 1) * MPAD] = total[
                at : at + CDEV
            ].astype(BF16)
    for block in range(12):
        lanes = slice(block * 128, block * 128 + 128)
        spatial = jnp.dot(modes[...], table_ref[:, lanes], preferred_element_type=F32)
        chip, inner = block // 3, block % 3
        for lat in range(LDEV):
            if block < 11:
                old = x_ref[lat, :, lanes].astype(F32)
            else:
                old = jnp.concatenate(
                    [x_ref[lat, :, 1408:1440], jnp.zeros((CDEV, 96), BF16)], axis=1
                ).astype(F32)
            new = (old + spatial[lat * CDEV : lat * CDEV + CDEV]).astype(BF16)
            if lat == 0:
                places = [(2 * chip, inner)]
            elif lat == 2:
                places = [(2 * chip + 1, inner)]
            elif inner < 2:
                places = [(2 * chip, 3 + inner)]
            else:
                places = [(2 * chip + 1, 3), (2 * chip + 1, 4)]
            for part, at in places:
                out_ref[part, :, at * 128 : at * 128 + 128] = new


def coef_kernel(coef_ref, out_ref, bias_ref):
    for k in range(BASIS):
        turned = jnp.concatenate([coef_ref[g, k] for g in range(CHANS)], axis=0).astype(F32).T
        if k == 1:
            bias_ref[...] = jnp.broadcast_to(
                jnp.sum(turned, axis=1, keepdims=True), bias_ref.shape
            )
        else:
            at = (k if k == 0 else k - 1) * 384
            out_ref[:, at : at + 384] = turned.astype(BF16)


def mixer_kernel(u_ref, coef_ref, bias_ref, out_ref):
    for block in range(5):
        lanes = slice(block * 128, block * 128 + 128)
        u = u_ref[:, lanes].astype(F32)
        t = jnp.tanh(u)
        base = 0.5 * u * (1.0 + jnp.tanh(0.5 * u))
        second = 2.0 * t * t - 1.0
        third = 2.0 * t * second - t
        fourth = 2.0 * t * third - second
        basis = jnp.concatenate(
            [piece.astype(BF16) for piece in (base, t, second, third, fourth)], axis=0
        )
        mixed = jnp.dot(coef_ref[...], basis, preferred_element_type=F32)
        out_ref[:, lanes] = (mixed + bias_ref[...]).astype(BF16)


def shards(state_field, slot_wave, spectral_filter, kan_coef):
    forward, inverse, weights, xrow, first, steps = make_tables()
    x = jnp.transpose(state_field, (1, 0, 2))
    slots = slot_wave.reshape(SPACES, SLOTS)
    cols = jnp.concatenate(
        [slots[:, :MAIN].T.reshape(-1)] + [slots[:, 16]] * 3 + [slots[:, 17]] * 3
    )
    cols = jnp.broadcast_to(cols[None, :], (8, COLS))
    coef_all = lax.all_gather(kan_coef, "chan")
    packed = pl.pallas_call(
        pack_kernel,
        out_shape=jax.ShapeDtypeStruct((SPACES * ROWS, 128), BF16),
        in_specs=[VMEM, VMEM, VMEM, SMEM],
        out_specs=VMEM,
        scratch_shapes=[
            pltpu.VMEM((288, MPAD), BF16),
            pltpu.VMEM((288, COLS), F32),
            pltpu.VMEM((SPACES * ROWS, 128), F32),
        ],
        compiler_params=PARAMS,
    )(x, forward, cols, weights)
    arrived = lax.all_to_all(
        packed.reshape(SPACES, ROWS, 128), "space", split_axis=0, concat_axis=0
    ).reshape(SPACES * ROWS, 128)
    legendre = pl.pallas_call(
        legendre_kernel,
        out_shape=jax.ShapeDtypeStruct((SLOTS, LMAX, 256), BF16),
        in_specs=[SMEM, SMEM, VMEM, VMEM],
        out_specs=VMEM,
        scratch_shapes=[
            pltpu.VMEM((2, LMAX * DEG_SLOTS, 128), F32),
            pltpu.VMEM((DEG_SLOTS, 128), jnp.int32),
            pltpu.VMEM((DEG_SLOTS, 256), F32),
        ],
        compiler_params=PARAMS,
        cost_estimate=pl.CostEstimate(flops=400_000_000, bytes_accessed=8_000_000, transcendentals=0),
    )(slot_wave, steps, xrow, first)
    coef, bias = pl.pallas_call(
        coef_kernel,
        out_shape=(
            jax.ShapeDtypeStruct((384, 5 * 384), BF16),
            jax.ShapeDtypeStruct((384, 128), F32),
        ),
        in_specs=[VMEM],
        out_specs=(VMEM, VMEM),
        compiler_params=PARAMS,
    )(coef_all)
    rebuilt = pl.pallas_call(
        spectral_kernel,
        out_shape=jax.ShapeDtypeStruct((SPACES * ROWS, 128), BF16),
        in_specs=[VMEM, VMEM, VMEM],
        out_specs=VMEM,
        scratch_shapes=[
            pltpu.VMEM((SPACES * ROWS, 128), F32),
            pltpu.VMEM((SLOTS, 96, 256), BF16),
            pltpu.VMEM((SLOTS, 96, 256), F32),
        ],
        compiler_params=PARAMS,
    )(arrived, legendre, spectral_filter)
    returned = lax.all_to_all(
        rebuilt.reshape(SPACES, ROWS, 128), "space", split_axis=0, concat_axis=0
    ).reshape(SPACES * ROWS, 128)
    updated = pl.pallas_call(
        inverse_kernel,
        out_shape=jax.ShapeDtypeStruct((CHANS, CDEV, PART), BF16),
        in_specs=[VMEM, VMEM, VMEM, VMEM],
        out_specs=VMEM,
        scratch_shapes=[
            pltpu.VMEM((SPACES * ROWS, 128), F32),
            pltpu.VMEM((288, COLS), BF16),
            pltpu.VMEM((144, 2 * MPAD), BF16),
        ],
        compiler_params=PARAMS,
    )(returned, inverse, cols, x)
    whole = lax.all_to_all(updated, "chan", split_axis=0, concat_axis=0).reshape(384, PART)
    mixed = pl.pallas_call(
        mixer_kernel,
        out_shape=jax.ShapeDtypeStruct((384, PART), BF16),
        in_specs=[VMEM, VMEM, VMEM],
        out_specs=VMEM,
        compiler_params=PARAMS,
    )(whole, coef, bias)
    back = lax.all_to_all(mixed.reshape(CHANS, CDEV, PART), "chan", split_axis=0, concat_axis=0)
    lats = []
    for lat in range(LDEV):
        blocks = []
        for chip in range(4):
            if lat == 0:
                blocks.append(back[2 * chip, :, 0:384])
            elif lat == 2:
                blocks.append(back[2 * chip + 1, :, 0:384])
            else:
                blocks.append(back[2 * chip, :, 384:640])
                blocks.append(back[2 * chip + 1, :, 384:512])
        lats.append(jnp.concatenate(blocks, axis=1)[:, :NLON])
    return jnp.stack(lats, axis=1)


def solution(mesh):
    in_specs = (
        P("chan", "space", None),
        P(),
        P("space", None, "chan", None),
        P(None, "chan", None),
    )
    out_specs = P("chan", "space", None)
    return jax.shard_map(shards, mesh=mesh, in_specs=in_specs, out_specs=out_specs, check_vma=False)
```

time: 418 us -> 151 us (0.36)
  the two profiles are of different devices: /device:TPU:8 before, /device:TPU:1 now
where the time goes in v1:
time: 151 us; the launch traced here: 150 us
  Pallas kernels  49.6 us (33%)
  blocking collectives  43.8 us (29%)
  starting transfers between devices  24.9 us (16%)
  waiting for transfers between devices  13.6 us (9%)
  between operations  13.5 us (9%)
  local copies, waits for them, and re-layouts  3.64 us (2%)
    all_to_all x1, blocking collectives, shards(): lax.all_to_all(rebuilt.reshape(SPACES, ROWS, 128), 'space', split_axis=0,...  30.5 us
    all_to_all x1, starting transfers between devices, shards(): lax.all_to_all(packed.reshape(SPACES, ROWS, 128), 'space', split_axis=0,...  17.1 us
    pallas_call x1, Pallas kernels, shards(): pl.pallas_call(spectral_kernel, out_shape=jax.ShapeDtypeStruct((SPACES *...  13.9 us
    pallas_call x1, Pallas kernels, shards(): pl.pallas_call(legendre_kernel, out_shape=jax.ShapeDtypeStruct((SLOTS, LM...  13.4 us
    all_to_all x1, blocking collectives, shards(): lax.all_to_all(mixed.reshape(CHANS, CDEV, PART), 'chan', split_axis=0, co...  13.3 us
    all_to_all x1, starting transfers between devices, shards(): lax.all_to_all(updated, 'chan', split_axis=0, concat_axis=0)  7.7 us
    pallas_call x1, Pallas kernels, shards(): pl.pallas_call(pack_kernel, out_shape=jax.ShapeDtypeStruct((SPACES * ROWS...  7.33 us
    pallas_call x1, Pallas kernels, shards(): pl.pallas_call(inverse_kernel, out_shape=jax.ShapeDtypeStruct((CHANS, CDE...  7.3 us
  transfers between devices with their start and end apart: 3, of which 2 were waited for; matrix products, arithmetic and copies ran while one was open for 0% of the time, Pallas kernels for 25%

profile of v1, /device:TPU:1, one launch (start us, length us, event | category | flops | bytes accessed | tf_op | source)
XLA Modules:
  0.0 149.8 jit_solution(17770047745913785239)
XLA Ops:
  6.5 0.8 reshape.25
  7.4 0.2 slice_reduce_fusion
  7.6 0.1 copy.12
  7.6 0.1 reshape.26
  7.7 0.1 concatenate.12
  7.8 0.6 broadcast_in_dim.2.cols_ref
  8.4 7.3 %shard_map.100 = bf16[3072,128]{1,0:T(8,128)(2,1)} custom-call(bf16[3,48,1440]{2,1,0:T(8,128)(2,1)} %bitcast.71, bf16[1440,1536]{1,0:T(8,128)(2,1)} %constant.12.clone.table_ref, s32[8,1408]{1,0:T(8,128)} %broadcast_in_dim.2.cols_ref, f32[192]{0:T(256)} %constant.13.clone.weight_ref), custom_call_target="tpu_custom_call" | custom-call | tf_op jit(solution)/shard_map/pallas_call | solution.py:299
  15.7 17.1 %all-to-all-start = ((bf16[64,48,128]{2,1,0:T(8,128)(2,1)}), bf16[64,48,128]{2,1,0:T(8,128)(2,1)S(1)}, u32[]{:S(2)}, u32[]{:S(2)}) async-start(bf16[64,48,128]{2,1,0:T(8,128)(2,1)} %bitcast.64), calls=%async_computation | async-start | bytes 1572864 | tf_op jit(solution)/shard_map/all_to_all | solution.py:311
  32.9 0.0 all-gather.3.cloned.1.call-start
  32.9 0.7 all-gather.3.cloned.1.call-update
  33.6 13.4 %shard_map.101.table_ref = bf16[18,720,256]{2,1,0:T(8,128)(2,1)} custom-call(s32[1152]{0:T(1024)} %wave_ref.1, f32[3,720]{1,0:T(4,128)} %constant.14.clone.steps_ref, f32[8,256]{1,0:T(8,128)} %constant.15.clone.x_ref, f32[728,256]{1,0:T(8,128)} %constant.16.clone.first_ref), custom_call_target="tpu_custom_call" | custom-call | flops 400000000 | bytes 8000000 | tf_op jit(solution)/shard_map/pallas_call | solution.py:314
  47.0 7.1 %all-to-all-done = bf16[64,48,128]{2,1,0:T(8,128)(2,1)S(1)} async-done(((bf16[64,48,128]{2,1,0:T(8,128)(2,1)}), bf16[64,48,128]{2,1,0:T(8,128)(2,1)S(1)}, u32[]{:S(2)}, u32[]{:S(2)}) %all-to-all-start) | async-done | bytes 786464 | tf_op jit(solution)/shard_map/all_to_all | solution.py:311
  54.1 0.0 copy-start
  54.1 0.9 copy-done
  54.9 13.9 %shard_map.102 = bf16[3072,128]{1,0:T(8,128)(2,1)} custom-call(bf16[3072,128]{1,0:T(8,128)(2,1)} %bitcast.66, bf16[18,720,256]{2,1,0:T(8,128)(2,1)} %shard_map.101.table_ref, bf16[18,2,48,720]{3,2,1,0:T(8,128)(2,1)} %gain_ref.1), custom_call_target="tpu_custom_call" | custom-call | tf_op jit(solution)/shard_map/pallas_call | solution.py:337
  68.8 30.5 %all_to_all.20 = bf16[64,48,128]{2,1,0:T(8,128)(2,1)} all-to-all(bf16[64,48,128]{2,1,0:T(8,128)(2,1)} %bitcast.67), channel_id=1, replica_groups=mesh['space'=64,'chan'=8] {'space'}, dimensions={0} | all-to-all | bytes 1572864 | tf_op jit(solution)/shard_map/all_to_all | solution.py:349
  99.3 7.3 %shard_map.103 = bf16[8,48,640]{2,1,0:T(8,128)(2,1)} custom-call(bf16[3072,128]{1,0:T(8,128)(2,1)} %bitcast.65, bf16[1536,1536]{1,0:T(8,128)(2,1)} %constant.17.clone.table_ref, s32[8,1408]{1,0:T(8,128)} %broadcast_in_dim.2.cols_ref, bf16[3,48,1440]{2,1,0:T(8,128)(2,1)} %bitcast.72), custom_call_target="tpu_custom_call" | custom-call | tf_op jit(solution)/shard_map/pallas_call | solution.py:352
  106.6 7.7 %all-to-all-start.2 = ((bf16[8,48,640]{2,1,0:T(8,128)(2,1)}), bf16[8,48,640]{2,1,0:T(8,128)(2,1)S(1)}, u32[]{:S(2)}, u32[]{:S(2)}) async-start(bf16[8,48,640]{2,1,0:T(8,128)(2,1)} %shard_map.103), calls=%async_computation.2 | async-start | bytes 983040 | tf_op jit(solution)/shard_map/all_to_all | solution.py:364
  114.3 0.0 all-gather.3.cloned.1.call-done
  114.3 3.3 %shard_map.104 = (bf16[384,1920]{1,0:T(8,128)(2,1)}, f32[384,128]{1,0:T(8,128)}) custom-call(bf16[8,6,48,384]{3,2,1,0:T(8,128)(2,1)} %bitcast.70), custom_call_target="tpu_custom_call" | custom-call | tf_op jit(solution)/shard_map/pallas_call | solution.py:327
  117.6 5.9 %all-to-all-done.2 = bf16[8,48,640]{2,1,0:T(8,128)(2,1)S(1)} async-done(((bf16[8,48,640]{2,1,0:T(8,128)(2,1)}), bf16[8,48,640]{2,1,0:T(8,128)(2,1)S(1)}, u32[]{:S(2)}, u32[]{:S(2)}) %all-to-all-start.2) | async-done | bytes 491552 | tf_op jit(solution)/shard_map/all_to_all | solution.py:364
  123.5 0.0 copy-start.1
  123.5 0.8 copy-done.1
  124.3 4.4 %shard_map.105 = bf16[384,640]{1,0:T(8,128)(2,1)} custom-call(bf16[384,640]{1,0:T(8,128)(2,1)} %bitcast.68, bf16[384,1920]{1,0:T(8,128)(2,1)} %get-tuple-element.7.coef_ref, f32[384,128]{1,0:T(8,128)} %get-tuple-element.8.bias_ref), custom_call_target="tpu_custom_call" | custom-call | tf_op jit(solution)/shard_map/pallas_call | solution.py:365
  128.6 13.3 %all_to_all.21 = bf16[8,48,640]{2,1,0:T(8,128)(2,1)S(1)} all-to-all(bf16[8,48,640]{2,1,0:T(8,128)(2,1)} %bitcast.69), channel_id=1, replica_groups=mesh['space'=64,'chan'=8] {'chan'}, dimensions={0} | all-to-all | bytes 983040 | tf_op jit(solution)/shard_map/all_to_all | solution.py:372
  142.1 0.8 pad_maximum_fusion
  (12 shorter events, 0.1 us)
Async XLA Ops:
  15.7 38.3 %all-to-all-start = ((bf16[64,48,128]{2,1,0:T(8,128)(2,1)}), bf16[64,48,128]{2,1,0:T(8,128)(2,1)S(1)}, u32[]{:S(2)}, u32[]{:S(2)}) async-start(bf16[64,48,128]{2,1,0:T(8,128)(2,1)} %bitcast.64), calls=%async_computation | async-start | bytes 1572864 | tf_op jit(solution)/shard_map/all_to_all | solution.py:311
  32.9 81.4 %all-gather.3.cloned.1.call-start = ((), (), s32[]{:S(2)}) async-start(), calls=%async_computation.4 | async-start | bytes 1990656 | tf_op jit(solution)/shard_map/all_gather | solution.py:298
  54.1 0.9 copy-start
  106.6 16.8 %all-to-all-start.2 = ((bf16[8,48,640]{2,1,0:T(8,128)(2,1)}), bf16[8,48,640]{2,1,0:T(8,128)(2,1)S(1)}, u32[]{:S(2)}, u32[]{:S(2)}) async-start(bf16[8,48,640]{2,1,0:T(8,128)(2,1)} %shard_map.103), calls=%async_computation.2 | async-start | bytes 983040 | tf_op jit(solution)/shard_map/all_to_all | solution.py:364
  123.5 0.8 copy-start.1
Sparse Core Ops, SparseCore 0:
  35.8 31.4 all-gather.2

commit v2 on v1

v2 whole, which is shorter than its diff:
```python
import math

import jax
import jax.numpy as jnp
import ml_dtypes
import numpy as np
from jax import lax
from jax.experimental import pallas as pl
from jax.experimental.pallas import tpu as pltpu
from jax.sharding import PartitionSpec as P

NLON = 1440
MMAX = 720
LMAX = 720
BASIS = 6
MPAD = 768
NPAD = 1536
SLOTS = 18
MAIN = 16
SPACES = 64
CHANS = 8
CDEV = 48
LDEV = 3
LAT = 192
ROWS = 48
COLS = 1408
PART = 640
DEG_SLOTS = 24
CHUNK = 240
F32 = jnp.float32
BF16 = jnp.bfloat16

VMEM = pl.BlockSpec(memory_space=pltpu.VMEM)
SMEM = pl.BlockSpec(memory_space=pltpu.SMEM)
HBM = pl.BlockSpec(memory_space=pl.ANY)
MESH = pl.DeviceIdType.MESH


def make_tables():
    m = np.arange(MMAX)[:, None]
    n = np.arange(NLON)[None, :]
    angle = (m * n % NLON) * (2.0 * np.pi / NLON)
    cos, sin = np.cos(angle), np.sin(angle)
    forward = np.zeros((2, NLON, MPAD))
    forward[0, :, :MMAX] = cos.T / NLON
    forward[1, :, :MMAX] = -sin.T / NLON
    factor = np.where(m == 0, 1.0, 2.0)
    inverse = np.zeros((2 * MPAD, NPAD))
    inverse[:MMAX, :NLON] = factor * cos
    inverse[MPAD : MPAD + MMAX, :NLON] = -factor * sin
    lat = np.arange(LAT)
    colat = 0.5 * np.pi + (lat + 0.5 - 0.5 * LAT) * (np.pi / LMAX)
    weights = (2.0 * np.pi * np.pi / LMAX * np.sin(colat)).astype(np.float32)
    order = (3 * np.arange(SPACES)[None, :] + np.arange(LDEV)[:, None]).reshape(-1)
    xrow = np.zeros((8, 256), np.float32)
    xrow[:, :LAT] = np.cos(colat)[order]
    first = np.zeros((MMAX + 8, 256), np.float32)
    for wave in range(MMAX):
        base = 0.5 * (
            math.log((2.0 * wave + 1.0) / (4.0 * math.pi))
            + math.lgamma(wave + 0.5)
            - math.lgamma(wave + 1.0)
            - 0.5 * math.log(math.pi)
        )
        first[wave, :LAT] = np.exp(base + wave * np.log(np.sin(colat)))[order]
    degree = np.arange(LMAX, dtype=np.float64)
    root = np.sqrt(np.maximum(4.0 * degree * degree - 1.0, 1.0))
    steps = np.stack([degree * degree, root, 1.0 / root]).astype(np.float32)
    return (
        forward.astype(ml_dtypes.bfloat16),
        inverse.astype(ml_dtypes.bfloat16),
        weights,
        xrow,
        first,
        steps,
    )


def one_hot(cols_row, start, size):
    waves = lax.broadcasted_iota(jnp.int32, (MPAD, size), 0)
    return jnp.where(waves == cols_row[0:1, start : start + size], 1.0, 0.0).astype(BF16)


def third_of(pair, shape):
    lane = lax.broadcasted_iota(jnp.int32, shape, 1)
    return jnp.where(lane >= 64, (2 * pair + 1) % 3, (2 * pair) % 3)


def far(i):
    return 4 + ((i + 1) // 2) * (1 - 2 * (i % 2))


def block_kernel(
    x_hbm,
    forward_hbm,
    inverse_hbm,
    gain_hbm,
    coef_hbm,
    wave_ref,
    weight_ref,
    steps_ref,
    cols_ref,
    xrow_ref,
    first_ref,
    out_ref,
    x_ref,
    forward_ref,
    inverse_ref,
    gain_ref,
    coefs,
    load_sem,
    send_sem,
    recv_sem,
    chan_send,
    chan_recv,
    hot,
    zonal,
    packed,
    rows,
    out_rows,
    in_rows,
    order_ref,
    start_ref,
    grown,
    legendre,
    spread,
    made,
    back_rows,
    got_rows,
    coef_ref,
    bias_ref,
    gathered,
    modes,
    updated,
    whole,
    mixed,
    final,
):
    here = lax.axis_index("space")
    group = lax.axis_index("chan")
    here_y, here_z = here // 8, here % 8

    def space_peer(k):
        return lax.rem(here_y + far(k // 8), 8) * 8 + lax.rem(here_z + far(k % 8), 8)

    loads = [
        pltpu.make_async_copy(source, target, load_sem.at[i])
        for i, (source, target) in enumerate(
            (
                (x_hbm, x_ref),
                (forward_hbm, forward_ref),
                (inverse_hbm, inverse_ref),
                (gain_hbm, gain_ref),
                (coef_hbm, coefs.at[group]),
            )
        )
    ]
    load_x, load_forward, load_inverse, load_gain, load_coef = loads
    for load in loads:
        load.start()

    barrier = pltpu.get_barrier_semaphore()

    def greet_space(k, carry):
        pl.semaphore_signal(
            barrier, inc=1, device_id={"space": space_peer(k)}, device_id_type=MESH
        )
        return carry

    def greet_chan(k, carry):
        pl.semaphore_signal(
            barrier, inc=1, device_id={"chan": lax.rem(group + k, CHANS)}, device_id_type=MESH
        )
        return carry

    lax.fori_loop(0, SPACES - 1, greet_space, 0)
    lax.fori_loop(1, CHANS, greet_chan, 0)

    def send_space(source, target, step, lat):
        def one(k, carry):
            peer = space_peer(k)
            pltpu.make_async_remote_copy(
                src_ref=source.at[lat, pl.ds(pl.multiple_of(peer * 16, 16), 16)],
                dst_ref=target.at[lat, pl.ds(pl.multiple_of(here * 16, 16), 16)],
                send_sem=send_sem.at[step, lat],
                recv_sem=recv_sem.at[step, lat],
                device_id={"space": peer},
                device_id_type=MESH,
            ).start()
            return carry

        lax.fori_loop(0, SPACES - 1, one, 0)
        own = pl.ds(pl.multiple_of(here * 16, 16), 16)
        target[lat, own, :] = source[lat, own, :]

    def wait_space(source, target, sem, step, lat):
        most = pl.ds(0, (SPACES - 1) * 16)
        pltpu.make_async_copy(
            source.at[lat, most], target.at[lat, most], sem.at[step, lat]
        ).wait()

    def send_chan(source, target, step):
        def one(k, carry):
            peer = lax.rem(group + far(k), CHANS)
            pltpu.make_async_remote_copy(
                src_ref=source.at[peer],
                dst_ref=target.at[group],
                send_sem=chan_send.at[step],
                recv_sem=chan_recv.at[step],
                device_id={"chan": peer},
                device_id_type=MESH,
            ).start()
            return carry

        lax.fori_loop(0, CHANS - 1, one, 0)
        target[group] = source[group]

    def wait_chan(source, target, sem, step):
        most = pl.ds(0, CHANS - 1)
        pltpu.make_async_copy(source.at[most], target.at[most], sem.at[step]).wait()

    cols = cols_ref[...]
    for start in range(0, COLS, 128):
        hot[:, start : start + 128] = one_hot(cols, start, 128)
    load_x.wait()
    load_forward.wait()
    for lat in range(LDEV):
        weight = weight_ref[here * LDEV + lat]
        for k in range(2):
            part = jnp.dot(x_ref[lat], forward_ref[k], preferred_element_type=F32)
            zonal[k * CDEV : k * CDEV + CDEV, :] = (part * weight).astype(BF16)
        packed[...] = jnp.dot(zonal[...], hot[...], preferred_element_type=F32)
        for pair in range(MAIN // 2):
            main = packed[:, pair * 128 : pair * 128 + 128]
            extra = jnp.zeros((32, 128), F32)
            if pair < 3:
                wide = packed[:, 1024 + pair * 128 : 1024 + pair * 128 + 128]
                third = third_of(pair, (32, 128))
                for th in range(3):
                    extra = jnp.where(third == th, wide[th * 32 : th * 32 + 32], extra)
            turned = jnp.concatenate([main, extra], axis=0).T
            for half in range(2):
                rows[lat, pl.ds(pair * 2 + half, 64, stride=16), :] = turned[
                    half * 64 : half * 64 + 64
                ]
        out_rows[lat] = rows[lat].astype(BF16)
        if lat == 0:
            pl.semaphore_wait(barrier, SPACES - 1 + CHANS - 1)
        send_space(out_rows, in_rows, 0, lat)

    load_coef.wait()

    def send_coef(k, carry):
        pltpu.make_async_remote_copy(
            src_ref=coefs.at[group],
            dst_ref=coefs.at[group],
            send_sem=chan_send.at[0],
            recv_sem=chan_recv.at[0],
            device_id={"chan": lax.rem(group + far(k), CHANS)},
            device_id_type=MESH,
        ).start()
        return carry

    lax.fori_loop(0, CHANS - 1, send_coef, 0)

    for slot in range(DEG_SLOTS):
        wave = wave_ref[here * SLOTS + slot] if slot < SLOTS else MMAX
        order_ref[slot : slot + 1, :] = jnp.full((1, 128), wave, jnp.int32)
        start_ref[slot : slot + 1, :] = first_ref[pl.ds(wave, 1), :]
    order = order_ref[...]
    square = order.astype(F32) * order.astype(F32)
    first_a, first_b = start_ref[:, 0:128], start_ref[:, 128:256]
    x_a = jnp.broadcast_to(xrow_ref[0:1, 0:128], (DEG_SLOTS, 128))
    x_b = jnp.broadcast_to(xrow_ref[0:1, 128:256], (DEG_SLOTS, 128))
    zero = jnp.zeros((DEG_SLOTS, 128), F32)
    state = (zero, zero, zero, zero, zero)
    for chunk in range(LMAX // CHUNK):

        def advance(block, carry, chunk=chunk):
            now_a, before_a, now_b, before_b, falling = carry
            for offset in range(8):
                at = block * 8 + offset
                degree = chunk * CHUNK + at
                gap = steps_ref[0, degree] - square
                inverse_root = lax.rsqrt(jnp.maximum(gap, 1.0))
                rising = steps_ref[1, degree] * inverse_root
                starts = order == degree
                next_a = jnp.where(starts, first_a, rising * (x_a * now_a - falling * before_a))
                next_b = jnp.where(starts, first_b, rising * (x_b * now_b - falling * before_b))
                falling = gap * inverse_root * steps_ref[2, degree]
                now_a, before_a, now_b, before_b = next_a, now_a, next_b, now_b
                grown[0, pl.ds(at * DEG_SLOTS, DEG_SLOTS), :] = next_a
                grown[1, pl.ds(at * DEG_SLOTS, DEG_SLOTS), :] = next_b
            return now_a, before_a, now_b, before_b, falling

        state = lax.fori_loop(0, CHUNK // 8, advance, state)

        def lay_out(slot, carry, chunk=chunk):
            for half in range(2):
                legendre[
                    slot, chunk * CHUNK : chunk * CHUNK + CHUNK, half * 128 : half * 128 + 128
                ] = grown[half, pl.ds(slot, CHUNK, stride=DEG_SLOTS), :].astype(BF16)
            return carry

        lax.fori_loop(0, SLOTS, lay_out, 0)

    for lat in range(LDEV):
        wait_space(out_rows, in_rows, recv_sem, 0, lat)
        rows[lat] = in_rows[lat].astype(F32)
    for row in range(MAIN):
        stack = jnp.concatenate(
            [rows[lat, pl.ds(row, 64, stride=16), :] for lat in range(LDEV)]
            + [jnp.zeros((64, 128), F32)],
            axis=0,
        )
        turned = stack.T.astype(BF16)
        spread[row] = turned[0:96]
        if row < 6:
            at = 32 * (row % 3)
            spread[MAIN + row // 3, at : at + 32, :] = turned[96:128]
    load_gain.wait()

    def filter_slot(slot, carry):
        table = legendre[slot]
        spectrum = lax.dot_general(
            spread[slot], table, (((1,), (1,)), ((), ())), preferred_element_type=F32
        )
        real, imag = spectrum[0:CDEV], spectrum[CDEV:96]
        gain_real = gain_ref[slot, 0].astype(F32)
        gain_imag = gain_ref[slot, 1].astype(F32)
        filtered = jnp.concatenate(
            [gain_real * real - gain_imag * imag, gain_real * imag + gain_imag * real], axis=0
        ).astype(BF16)
        made[slot] = jnp.dot(filtered, table, preferred_element_type=F32)
        return carry

    lax.fori_loop(0, SLOTS, filter_slot, 0)
    for row in range(MAIN):
        extra = jnp.zeros((32, 256), F32)
        if row < 6:
            at = 32 * (row % 3)
            extra = made[MAIN + row // 3, at : at + 32, :]
        turned = jnp.concatenate([made[row], extra], axis=0).T
        for lat in range(LDEV):
            rows[lat, pl.ds(row, 64, stride=16), :] = turned[lat * 64 : lat * 64 + 64]
    for lat in range(LDEV):
        back_rows[lat] = rows[lat].astype(BF16)
        send_space(back_rows, got_rows, 1, lat)

    pltpu.make_async_copy(
        coefs.at[pl.ds(0, CHANS - 1)], coefs.at[pl.ds(0, CHANS - 1)], chan_recv.at[0]
    ).wait()
    for k in range(BASIS):
        turned = jnp.concatenate([coefs[g, k] for g in range(CHANS)], axis=0).astype(F32).T
        if k == 1:
            bias_ref[...] = jnp.broadcast_to(
                jnp.sum(turned, axis=1, keepdims=True), bias_ref.shape
            )
        else:
            at = (k if k == 0 else k - 1) * 384
            coef_ref[:, at : at + 384] = turned.astype(BF16)
    load_inverse.wait()

    for lat in range(LDEV):
        wait_space(back_rows, got_rows, recv_sem, 1, lat)
        rows[lat] = got_rows[lat].astype(F32)
        for pair in range(MAIN // 2):
            turned = jnp.concatenate(
                [rows[lat, pl.ds(pair * 2 + half, 64, stride=16), :] for half in range(2)], axis=0
            ).T
            gathered[:, pair * 128 : pair * 128 + 128] = turned[0:96].astype(BF16)
            if pair < 3:
                third = third_of(pair, (32, 128))
                for th in range(3):
                    gathered[
                        th * 32 : th * 32 + 32, 1024 + pair * 128 : 1024 + pair * 128 + 128
                    ] = jnp.where(third == th, turned[96:128], 0.0).astype(BF16)
        total = lax.dot_general(
            gathered[...], hot[...], (((1,), (1,)), ((), ())), preferred_element_type=F32
        )
        for k in range(2):
            modes[:, k * MPAD : (k + 1) * MPAD] = total[k * CDEV : k * CDEV + CDEV].astype(BF16)
        for block in range(12):
            lanes = slice(block * 128, block * 128 + 128)
            spatial = jnp.dot(modes[...], inverse_ref[:, lanes], preferred_element_type=F32)
            chip, inner = block // 3, block % 3
            if block < 11:
                old = x_ref[lat, :, lanes].astype(F32)
            else:
                old = jnp.concatenate(
                    [x_ref[lat, :, 1408:1440], jnp.zeros((CDEV, 96), BF16)], axis=1
                ).astype(F32)
            new = (old + spatial).astype(BF16)
            if lat == 0:
                places = [(2 * chip, inner)]
            elif lat == 2:
                places = [(2 * chip + 1, inner)]
            elif inner < 2:
                places = [(2 * chip, 3 + inner)]
            else:
                places = [(2 * chip + 1, 3), (2 * chip + 1, 4)]
            for part, at in places:
                updated[part, :, at * 128 : at * 128 + 128] = new
    send_chan(updated, whole, 1)
    wait_chan(updated, whole, chan_recv, 1)

    for block in range(5):
        lanes = slice(block * 128, block * 128 + 128)
        u = whole[:, :, lanes].reshape(384, 128).astype(F32)
        t = jnp.tanh(u)
        base = 0.5 * u * (1.0 + jnp.tanh(0.5 * u))
        second = 2.0 * t * t - 1.0
        third = 2.0 * t * second - t
        fourth = 2.0 * t * third - second
        basis = jnp.concatenate(
            [piece.astype(BF16) for piece in (base, t, second, third, fourth)], axis=0
        )
        total = jnp.dot(coef_ref[...], basis, preferred_element_type=F32)
        mixed[:, :, lanes] = (total + bias_ref[...]).astype(BF16).reshape(CHANS, CDEV, 128)
    send_chan(mixed, final, 2)
    wait_chan(mixed, final, chan_recv, 2)
    for block in range(12):
        chip, inner = block // 3, block % 3
        width = 128 if block < 11 else 32
        for lat in range(LDEV):
            if lat == 0:
                part, at = 2 * chip, inner
            elif lat == 2:
                part, at = 2 * chip + 1, inner
            elif inner < 2:
                part, at = 2 * chip, 3 + inner
            else:
                part, at = 2 * chip + 1, 3
            out_ref[lat, :, block * 128 : block * 128 + width] = final[
                part, :, at * 128 : at * 128 + width
            ]

    for lat in range(LDEV):
        wait_space(out_rows, in_rows, send_sem, 0, lat)
        wait_space(back_rows, got_rows, send_sem, 1, lat)
    pltpu.make_async_copy(
        coefs.at[pl.ds(0, CHANS - 1)], coefs.at[pl.ds(0, CHANS - 1)], chan_send.at[0]
    ).wait()
    wait_chan(updated, whole, chan_send, 1)
    wait_chan(mixed, final, chan_send, 2)


def shards(state_field, slot_wave, spectral_filter, kan_coef):
    forward, inverse, weights, xrow, first, steps = make_tables()
    x = jnp.transpose(state_field, (1, 0, 2))
    slots = slot_wave.reshape(SPACES, SLOTS)
    cols = jnp.concatenate(
        [slots[:, :MAIN].T.reshape(-1)] + [slots[:, 16]] * 3 + [slots[:, 17]] * 3
    )
    cols = jnp.broadcast_to(cols[None, :], (8, COLS))
    message = pltpu.VMEM((LDEV, SPACES * 16, 128), BF16)
    part = pltpu.VMEM((CHANS, CDEV, PART), BF16)
    out = pl.pallas_call(
        block_kernel,
        out_shape=jax.ShapeDtypeStruct((LDEV, CDEV, NLON), BF16),
        in_specs=[HBM] * 5 + [SMEM] * 3 + [VMEM] * 3,
        out_specs=VMEM,
        scratch_shapes=[
            pltpu.VMEM((LDEV, CDEV, NLON), BF16),
            pltpu.VMEM((2, NLON, MPAD), BF16),
            pltpu.VMEM((2 * MPAD, NPAD), BF16),
            pltpu.VMEM((SLOTS, 2, CDEV, LMAX), BF16),
            pltpu.VMEM((CHANS, BASIS, CDEV, 384), BF16),
            pltpu.SemaphoreType.DMA((5,)),
            pltpu.SemaphoreType.DMA((2, LDEV)),
            pltpu.SemaphoreType.DMA((2, LDEV)),
            pltpu.SemaphoreType.DMA((3,)),
            pltpu.SemaphoreType.DMA((3,)),
            pltpu.VMEM((MPAD, COLS), BF16),
            pltpu.VMEM((96, MPAD), BF16),
            pltpu.VMEM((96, COLS), F32),
            pltpu.VMEM((LDEV, SPACES * 16, 128), F32),
            message,
            message,
            pltpu.VMEM((DEG_SLOTS, 128), jnp.int32),
            pltpu.VMEM((DEG_SLOTS, 256), F32),
            pltpu.VMEM((2, CHUNK * DEG_SLOTS, 128), F32),
            pltpu.VMEM((SLOTS, LMAX, 256), BF16),
            pltpu.VMEM((SLOTS, 96, 256), BF16),
            pltpu.VMEM((SLOTS, 96, 256), F32),
            message,
            message,
            pltpu.VMEM((384, 5 * 384), BF16),
            pltpu.VMEM((384, 128), F32),
            pltpu.VMEM((96, COLS), BF16),
            pltpu.VMEM((CDEV, 2 * MPAD), BF16),
            part,
            part,
            part,
            part,
        ],
        compiler_params=pltpu.CompilerParams(
            collective_id=0, has_side_effects=True, vmem_limit_bytes=60 * 1024 * 1024
        ),
        name="spectral_block",
    )(x, forward, inverse, spectral_filter, kan_coef, slot_wave, weights, steps, cols, xrow, first)
    return jnp.transpose(out, (1, 0, 2))


def solution(mesh):
    in_specs = (
        P("chan", "space", None),
        P(),
        P("space", None, "chan", None),
        P(None, "chan", None),
    )
    out_specs = P("chan", "space", None)
    return jax.shard_map(shards, mesh=mesh, in_specs=in_specs, out_specs=out_specs, check_vma=False)
```

time: 151 us -> 93.1 us (0.62)
  blocking collectives: 43.8 us -> 0 us
  Pallas kernels: 49.6 us -> 89.2 us
  starting transfers between devices: 24.9 us -> 0 us
  waiting for transfers between devices: 13.6 us -> 0 us
  between operations: 13.5 us -> 0.02 us
    all_to_all x2 -> x0, blocking collectives: 43.8 us -> none  [the longest x1 30.5 us: shards(): lax.all_to_all(rebuilt.reshape(SPACES, ROWS, 128), 'space', split_axis=0,...]
    pallas_call x6 -> x1, Pallas kernels: 49.6 us -> 89.2 us  [shards(): pl.pallas_call(block_kernel, out_shape=jax.ShapeDtypeStruct((LDEV, CDEV,...]
    all_to_all x2 -> x0, starting transfers between devices: 24.8 us -> none  [the longest x1 17.1 us: shards(): lax.all_to_all(packed.reshape(SPACES, ROWS, 128), 'space', split_axis=0,...]
    all_to_all x2 -> x0, waiting for transfers between devices: 12.9 us -> none  [the longest x1 7.06 us: shards(): lax.all_to_all(packed.reshape(SPACES, ROWS, 128), 'space', split_axis=0,...]
  transfers between devices with their start and end apart: 3 -> 0, of which waited for: 2 -> 0; matrix products, arithmetic and copies ran while one was open for 0% -> 0% of each run, Pallas kernels for 25% -> 0%
where the time goes in v2:
time: 93.1 us; the launch traced here: 92.8 us
  Pallas kernels  89.2 us (96%)
  local copies, waits for them, and re-layouts  3.66 us (4%)
    pallas_call x1, Pallas kernels, shards(): pl.pallas_call(block_kernel, out_shape=jax.ShapeDtypeStruct((LDEV, CDEV,...  89.2 us

profile of v2, /device:TPU:1, one launch (start us, length us, event | category | flops | bytes accessed | tf_op | source)
XLA Modules:
  0.0 92.8 jit_solution(7814073886704177669)
XLA Ops:
  0.0 0.8 reshape.7
  0.8 0.2 slice_reduce_fusion
  1.0 0.1 copy.11
  1.1 0.1 reshape.8
  1.2 0.1 concatenate.3
  1.2 0.6 broadcast_in_dim.2.cols_ref
  1.9 89.2 %spectral_block.1 = bf16[3,48,1440]{2,1,0:T(8,128)(2,1)} custom-call(bf16[3,48,1440]{2,1,0:T(8,128)(2,1)} %bitcast.5, bf16[2,1440,768]{2,1,0:T(8,128)(2,1)} %constant.12.clone.forward_hbm, bf16[1536,1536]{1,0:T(8,128)(2,1)} %constant.13.clone.inverse_hbm, bf16[18,2,48,720]{3,2,1,0:T(8,128)(2,1)} %gain_hbm.1, bf16[6,48,384]{2,1,0:T(8,128)(2,1)} %coef_hbm.1, ...), custom_call_target="tpu_custom_call" | custom-call | tf_op jit(solution)/shard_map/spectral_block/pallas_call | solution.py:458
  91.0 1.8 %copy.13 = bf16[48,3,1440]{2,0,1:T(8,128)(2,1)} copy(bf16[48,3,1440]{2,0,1:T(8,128)(2,1)} %bitcast.4) | data formatting | bytes 829440
  (1 shorter events, 0.0 us)

commit v3 on v2

--- a/solution.py
+++ b/solution.py
@@ -24,7 +24,7 @@
 LAT = 192
 ROWS = 48
 COLS = 1408
-PART = 640
+PART = 256
 DEG_SLOTS = 24
 CHUNK = 240
 F32 = jnp.float32
@@ -90,6 +90,13 @@
     return 4 + ((i + 1) // 2) * (1 - 2 * (i % 2))
 
 
+def places(lat, block):
+    chip, inner = block // 3, block % 3
+    if lat == 1:
+        return [[(2 * chip, 0), (2 * chip, 1)], [(2 * chip + 1, 0)], [(2 * chip + 1, 1)]][inner]
+    return [[(2 * chip, 0)], [(2 * chip, 1)], [(2 * chip + 1, 0), (2 * chip + 1, 1)]][inner]
+
+
 def block_kernel(
     x_hbm,
     forward_hbm,
@@ -113,6 +120,8 @@
     recv_sem,
     chan_send,
     chan_recv,
+    coef_send,
+    coef_recv,
     hot,
     zonal,
     packed,
@@ -131,6 +140,7 @@
     bias_ref,
     gathered,
     modes,
+    basis,
     updated,
     whole,
     mixed,
@@ -139,6 +149,8 @@
     here = lax.axis_index("space")
     group = lax.axis_index("chan")
     here_y, here_z = here // 8, here % 8
+    chip, core = group // 2, group % 2
+    sibling = chip * 2 + 1 - core
 
     def space_peer(k):
         return lax.rem(here_y + far(k // 8), 8) * 8 + lax.rem(here_z + far(k % 8), 8)
@@ -151,7 +163,7 @@
                 (forward_hbm, forward_ref),
                 (inverse_hbm, inverse_ref),
                 (gain_hbm, gain_ref),
-                (coef_hbm, coefs.at[group]),
+                (coef_hbm, coefs.at[core, chip]),
             )
         )
     ]
@@ -199,25 +211,42 @@
             source.at[lat, most], target.at[lat, most], sem.at[step, lat]
         ).wait()
 
-    def send_chan(source, target, step):
+    def send_chan(source, target, step, lat):
         def one(k, carry):
             peer = lax.rem(group + far(k), CHANS)
             pltpu.make_async_remote_copy(
-                src_ref=source.at[peer],
-                dst_ref=target.at[group],
-                send_sem=chan_send.at[step],
-                recv_sem=chan_recv.at[step],
+                src_ref=source.at[lat, peer],
+                dst_ref=target.at[lat, group],
+                send_sem=chan_send.at[step, lat],
+                recv_sem=chan_recv.at[step, lat],
                 device_id={"chan": peer},
                 device_id_type=MESH,
             ).start()
             return carry
 
         lax.fori_loop(0, CHANS - 1, one, 0)
-        target[group] = source[group]
-
-    def wait_chan(source, target, sem, step):
+        target[lat, group] = source[lat, group]
+
+    def wait_chan(source, target, sem, step, lat):
         most = pl.ds(0, CHANS - 1)
-        pltpu.make_async_copy(source.at[most], target.at[most], sem.at[step]).wait()
+        pltpu.make_async_copy(
+            source.at[lat, most], target.at[lat, most], sem.at[step, lat]
+        ).wait()
+
+    def send_coef(k, carry):
+        pltpu.make_async_remote_copy(
+            src_ref=coefs.at[core, chip],
+            dst_ref=coefs.at[core, chip],
+            send_sem=coef_send.at[0],
+            recv_sem=coef_recv.at[0],
+            device_id={"chan": lax.rem(group + 2 * k, CHANS)},
+            device_id_type=MESH,
+        ).start()
+        return carry
+
+    def wait_coef(count, sem):
+        most = pl.ds(0, count)
+        pltpu.make_async_copy(coefs.at[0, most], coefs.at[0, most], sem).wait()
 
     cols = cols_ref[...]
     for start in range(0, COLS, 128):
@@ -247,21 +276,10 @@
         if lat == 0:
             pl.semaphore_wait(barrier, SPACES - 1 + CHANS - 1)
         send_space(out_rows, in_rows, 0, lat)
-
-    load_coef.wait()
-
-    def send_coef(k, carry):
-        pltpu.make_async_remote_copy(
-            src_ref=coefs.at[group],
-            dst_ref=coefs.at[group],
-            send_sem=chan_send.at[0],
-            recv_sem=chan_recv.at[0],
-            device_id={"chan": lax.rem(group + far(k), CHANS)},
-            device_id_type=MESH,
-        ).start()
-        return carry
-
-    lax.fori_loop(0, CHANS - 1, send_coef, 0)
+        if lat == 0:
+            load_coef.wait()
+            lax.fori_loop(1, 4, send_coef, 0)
+
 
     for slot in range(DEG_SLOTS):
         wave = wave_ref[here * SLOTS + slot] if slot < SLOTS else MMAX
@@ -304,6 +322,16 @@
 
         lax.fori_loop(0, SLOTS, lay_out, 0)
 
+    wait_coef(3, coef_recv.at[0])
+    pltpu.make_async_remote_copy(
+        src_ref=coefs.at[core],
+        dst_ref=coefs.at[core],
+        send_sem=coef_send.at[1],
+        recv_sem=coef_recv.at[1],
+        device_id={"chan": sibling},
+        device_id_type=MESH,
+    ).start()
+
     for lat in range(LDEV):
         wait_space(out_rows, in_rows, recv_sem, 0, lat)
         rows[lat] = in_rows[lat].astype(F32)
@@ -320,21 +348,25 @@
             spread[MAIN + row // 3, at : at + 32, :] = turned[96:128]
     load_gain.wait()
 
-    def filter_slot(slot, carry):
-        table = legendre[slot]
-        spectrum = lax.dot_general(
-            spread[slot], table, (((1,), (1,)), ((), ())), preferred_element_type=F32
-        )
-        real, imag = spectrum[0:CDEV], spectrum[CDEV:96]
-        gain_real = gain_ref[slot, 0].astype(F32)
-        gain_imag = gain_ref[slot, 1].astype(F32)
-        filtered = jnp.concatenate(
-            [gain_real * real - gain_imag * imag, gain_real * imag + gain_imag * real], axis=0
-        ).astype(BF16)
-        made[slot] = jnp.dot(filtered, table, preferred_element_type=F32)
+    def filter_slots(step, carry):
+        slots = [step * 3 + i for i in range(3)]
+        spectra = [
+            lax.dot_general(
+                spread[slot], legendre[slot], (((1,), (1,)), ((), ())), preferred_element_type=F32
+            )
+            for slot in slots
+        ]
+        for slot, spectrum in zip(slots, spectra):
+            real, imag = spectrum[0:CDEV], spectrum[CDEV:96]
+            gain_real = gain_ref[slot, 0].astype(F32)
+            gain_imag = gain_ref[slot, 1].astype(F32)
+            filtered = jnp.concatenate(
+                [gain_real * real - gain_imag * imag, gain_real * imag + gain_imag * real], axis=0
+            ).astype(BF16)
+            made[slot] = jnp.dot(filtered, legendre[slot], preferred_element_type=F32)
         return carry
 
-    lax.fori_loop(0, SLOTS, filter_slot, 0)
+    lax.fori_loop(0, SLOTS // 3, filter_slots, 0)
     for row in range(MAIN):
         extra = jnp.zeros((32, 256), F32)
         if row < 6:
@@ -347,11 +379,11 @@
         back_rows[lat] = rows[lat].astype(BF16)
         send_space(back_rows, got_rows, 1, lat)
 
-    pltpu.make_async_copy(
-        coefs.at[pl.ds(0, CHANS - 1)], coefs.at[pl.ds(0, CHANS - 1)], chan_recv.at[0]
-    ).wait()
+    wait_coef(4, coef_recv.at[1])
     for k in range(BASIS):
-        turned = jnp.concatenate([coefs[g, k] for g in range(CHANS)], axis=0).astype(F32).T
+        turned = jnp.concatenate(
+            [coefs[g % 2, g // 2, k] for g in range(CHANS)], axis=0
+        ).astype(F32).T
         if k == 1:
             bias_ref[...] = jnp.broadcast_to(
                 jnp.sum(turned, axis=1, keepdims=True), bias_ref.shape
@@ -360,6 +392,26 @@
             at = (k if k == 0 else k - 1) * 384
             coef_ref[:, at : at + 384] = turned.astype(BF16)
     load_inverse.wait()
+
+    def mix(lat):
+        wait_chan(updated, whole, chan_recv, 0, lat)
+        u = whole[lat].reshape(384, PART).astype(F32)
+        t = jnp.tanh(u)
+        base = 0.5 * u * (1.0 + jnp.tanh(0.5 * u))
+        second = 2.0 * t * t - 1.0
+        third = 2.0 * t * second - t
+        fourth = 2.0 * t * third - second
+        for k, piece in enumerate((base, t, second, third, fourth)):
+            basis[k * 384 : k * 384 + 384, :] = piece.astype(BF16)
+        for half in range(2):
+            total = jnp.dot(
+                coef_ref[half * 192 : half * 192 + 192, :], basis[...], preferred_element_type=F32
+            )
+            bias = bias_ref[half * 192 : half * 192 + 192, 0:1]
+            mixed[lat, half * 4 : half * 4 + 4] = (
+                (total + bias).astype(BF16).reshape(4, CDEV, PART)
+            )
+        send_chan(mixed, final, 1, lat)
 
     for lat in range(LDEV):
         wait_space(back_rows, got_rows, recv_sem, 1, lat)
@@ -380,69 +432,44 @@
         )
         for k in range(2):
             modes[:, k * MPAD : (k + 1) * MPAD] = total[k * CDEV : k * CDEV + CDEV].astype(BF16)
+        for strip in range(6):
+            spatial = jnp.dot(
+                modes[...],
+                inverse_ref[:, strip * 256 : strip * 256 + 256],
+                preferred_element_type=F32,
+            )
+            for block in (2 * strip, 2 * strip + 1):
+                lanes = slice(block * 128, block * 128 + 128)
+                if block < 11:
+                    old = x_ref[lat, :, lanes].astype(F32)
+                else:
+                    old = jnp.concatenate(
+                        [x_ref[lat, :, 1408:1440], jnp.zeros((CDEV, 96), BF16)], axis=1
+                    ).astype(F32)
+                at = (block % 2) * 128
+                new = (old + spatial[:, at : at + 128]).astype(BF16)
+                for part, place in places(lat, block):
+                    updated[lat, part, :, place * 128 : place * 128 + 128] = new
+        send_chan(updated, whole, 0, lat)
+        if lat > 0:
+            mix(lat - 1)
+    mix(LDEV - 1)
+    for lat in range(LDEV):
+        wait_chan(mixed, final, chan_recv, 1, lat)
         for block in range(12):
-            lanes = slice(block * 128, block * 128 + 128)
-            spatial = jnp.dot(modes[...], inverse_ref[:, lanes], preferred_element_type=F32)
-            chip, inner = block // 3, block % 3
-            if block < 11:
-                old = x_ref[lat, :, lanes].astype(F32)
-            else:
-                old = jnp.concatenate(
-                    [x_ref[lat, :, 1408:1440], jnp.zeros((CDEV, 96), BF16)], axis=1
-                ).astype(F32)
-            new = (old + spatial).astype(BF16)
-            if lat == 0:
-                places = [(2 * chip, inner)]
-            elif lat == 2:
-                places = [(2 * chip + 1, inner)]
-            elif inner < 2:
-                places = [(2 * chip, 3 + inner)]
-            else:
-                places = [(2 * chip + 1, 3), (2 * chip + 1, 4)]
-            for part, at in places:
-                updated[part, :, at * 128 : at * 128 + 128] = new
-    send_chan(updated, whole, 1)
-    wait_chan(updated, whole, chan_recv, 1)
-
-    for block in range(5):
-        lanes = slice(block * 128, block * 128 + 128)
-        u = whole[:, :, lanes].reshape(384, 128).astype(F32)
-        t = jnp.tanh(u)
-        base = 0.5 * u * (1.0 + jnp.tanh(0.5 * u))
-        second = 2.0 * t * t - 1.0
-        third = 2.0 * t * second - t
-        fourth = 2.0 * t * third - second
-        basis = jnp.concatenate(
-            [piece.astype(BF16) for piece in (base, t, second, third, fourth)], axis=0
-        )
-        total = jnp.dot(coef_ref[...], basis, preferred_element_type=F32)
-        mixed[:, :, lanes] = (total + bias_ref[...]).astype(BF16).reshape(CHANS, CDEV, 128)
-    send_chan(mixed, final, 2)
-    wait_chan(mixed, final, chan_recv, 2)
-    for block in range(12):
-        chip, inner = block // 3, block % 3
-        width = 128 if block < 11 else 32
-        for lat in range(LDEV):
-            if lat == 0:
-                part, at = 2 * chip, inner
-            elif lat == 2:
-                part, at = 2 * chip + 1, inner
-            elif inner < 2:
-                part, at = 2 * chip, 3 + inner
-            else:
-                part, at = 2 * chip + 1, 3
+            part, place = places(lat, block)[0]
+            width = 128 if block < 11 else 32
             out_ref[lat, :, block * 128 : block * 128 + width] = final[
-                part, :, at * 128 : at * 128 + width
+                lat, part, :, place * 128 : place * 128 + width
             ]
 
     for lat in range(LDEV):
         wait_space(out_rows, in_rows, send_sem, 0, lat)
         wait_space(back_rows, got_rows, send_sem, 1, lat)
-    pltpu.make_async_copy(
-        coefs.at[pl.ds(0, CHANS - 1)], coefs.at[pl.ds(0, CHANS - 1)], chan_send.at[0]
-    ).wait()
-    wait_chan(updated, whole, chan_send, 1)
-    wait_chan(mixed, final, chan_send, 2)
+        wait_chan(updated, whole, chan_send, 0, lat)
+        wait_chan(mixed, final, chan_send, 1, lat)
+    wait_coef(3, coef_send.at[0])
+    wait_coef(4, coef_send.at[1])
 
 
 def shards(state_field, slot_wave, spectral_filter, kan_coef):
@@ -454,7 +481,7 @@
     )
     cols = jnp.broadcast_to(cols[None, :], (8, COLS))
     message = pltpu.VMEM((LDEV, SPACES * 16, 128), BF16)
-    part = pltpu.VMEM((CHANS, CDEV, PART), BF16)
+    part = pltpu.VMEM((LDEV, CHANS, CDEV, PART), BF16)
     out = pl.pallas_call(
         block_kernel,
         out_shape=jax.ShapeDtypeStruct((LDEV, CDEV, NLON), BF16),
@@ -465,12 +492,14 @@
             pltpu.VMEM((2, NLON, MPAD), BF16),
             pltpu.VMEM((2 * MPAD, NPAD), BF16),
             pltpu.VMEM((SLOTS, 2, CDEV, LMAX), BF16),
-            pltpu.VMEM((CHANS, BASIS, CDEV, 384), BF16),
+            pltpu.VMEM((2, CHANS // 2, BASIS, CDEV, 384), BF16),
             pltpu.SemaphoreType.DMA((5,)),
             pltpu.SemaphoreType.DMA((2, LDEV)),
             pltpu.SemaphoreType.DMA((2, LDEV)),
-            pltpu.SemaphoreType.DMA((3,)),
-            pltpu.SemaphoreType.DMA((3,)),
+            pltpu.SemaphoreType.DMA((2, LDEV)),
+            pltpu.SemaphoreType.DMA((2, LDEV)),
+            pltpu.SemaphoreType.DMA((2,)),
+            pltpu.SemaphoreType.DMA((2,)),
             pltpu.VMEM((MPAD, COLS), BF16),
             pltpu.VMEM((96, MPAD), BF16),
             pltpu.VMEM((96, COLS), F32),
@@ -489,6 +518,7 @@
             pltpu.VMEM((384, 128), F32),
             pltpu.VMEM((96, COLS), BF16),
             pltpu.VMEM((CDEV, 2 * MPAD), BF16),
+            pltpu.VMEM((5 * 384, PART), BF16),
             part,
             part,
             part,

time: 93.1 us -> 84.5 us (0.908)
  Pallas kernels: 89.2 us -> 80.6 us
    pallas_call x1, Pallas kernels: 89.2 us -> 80.6 us  [shards(): pl.pallas_call(block_kernel, out_shape=jax.ShapeDtypeStruct((LDEV, CDEV,...]
where the time goes in v3:
time: 84.5 us; the launch traced here: 84.2 us
  Pallas kernels  80.6 us (95%)
  local copies, waits for them, and re-layouts  3.66 us (4%)
    pallas_call x1, Pallas kernels, shards(): pl.pallas_call(block_kernel, out_shape=jax.ShapeDtypeStruct((LDEV, CDEV,...  80.6 us
    unnamed x1, local copies, waits for them, and re-layouts  1.8 us

profile of v3, /device:TPU:1, one launch (start us, length us, event | category | flops | bytes accessed | tf_op | source)
XLA Modules:
  0.0 84.2 jit_solution(18159335707128086823)
XLA Ops:
  0.0 0.8 reshape.7
  0.8 0.2 slice_reduce_fusion
  1.0 0.1 copy.11
  1.1 0.1 reshape.8
  1.2 0.1 concatenate.3
  1.2 0.6 broadcast_in_dim.2.cols_ref
  1.9 80.6 %spectral_block.1 = bf16[3,48,1440]{2,1,0:T(8,128)(2,1)} custom-call(bf16[3,48,1440]{2,1,0:T(8,128)(2,1)} %bitcast.5, bf16[2,1440,768]{2,1,0:T(8,128)(2,1)} %constant.12.clone.forward_hbm, bf16[1536,1536]{1,0:T(8,128)(2,1)} %constant.13.clone.inverse_hbm, bf16[18,2,48,720]{3,2,1,0:T(8,128)(2,1)} %gain_hbm.1, bf16[6,48,384]{2,1,0:T(8,128)(2,1)} %coef_hbm.1, ...), custom_call_target="tpu_custom_call" | custom-call | tf_op jit(solution)/shard_map/spectral_block/pallas_call | solution.py:485
  82.4 1.8 %copy.13 = bf16[48,3,1440]{2,0,1:T(8,128)(2,1)} copy(bf16[48,3,1440]{2,0,1:T(8,128)(2,1)} %bitcast.4) | data formatting | bytes 829440
  (1 shorter events, 0.0 us)

commit v4 on v3

--- a/solution.py
+++ b/solution.py
@@ -23,7 +23,7 @@
 LDEV = 3
 LAT = 192
 ROWS = 48
-COLS = 1408
+COLS = 1152
 PART = 256
 DEG_SLOTS = 24
 CHUNK = 240
@@ -81,9 +81,10 @@
     return jnp.where(waves == cols_row[0:1, start : start + size], 1.0, 0.0).astype(BF16)
 
 
-def third_of(pair, shape):
-    lane = lax.broadcasted_iota(jnp.int32, shape, 1)
-    return jnp.where(lane >= 64, (2 * pair + 1) % 3, (2 * pair) % 3)
+ORDER = sorted(
+    ((k // 8, k % 8) for k in range(1, SPACES)),
+    key=lambda step: -min(step[0], 8 - step[0]) - min(step[1], 8 - step[1]),
+)
 
 
 def far(i):
@@ -109,7 +110,7 @@
     cols_ref,
     xrow_ref,
     first_ref,
-    out_ref,
+    final,
     x_ref,
     forward_ref,
     inverse_ref,
@@ -125,6 +126,7 @@
     hot,
     zonal,
     packed,
+    flat,
     rows,
     out_rows,
     in_rows,
@@ -144,7 +146,6 @@
     updated,
     whole,
     mixed,
-    final,
 ):
     here = lax.axis_index("space")
     group = lax.axis_index("chan")
@@ -168,8 +169,8 @@
         )
     ]
     load_x, load_forward, load_inverse, load_gain, load_coef = loads
-    for load in loads:
-        load.start()
+    load_x.start()
+    load_forward.start()
 
     barrier = pltpu.get_barrier_semaphore()
 
@@ -189,8 +190,8 @@
     lax.fori_loop(1, CHANS, greet_chan, 0)
 
     def send_space(source, target, step, lat):
-        def one(k, carry):
-            peer = space_peer(k)
+        for oy, oz in ORDER:
+            peer = lax.rem(here_y + oy, 8) * 8 + lax.rem(here_z + oz, 8)
             pltpu.make_async_remote_copy(
                 src_ref=source.at[lat, pl.ds(pl.multiple_of(peer * 16, 16), 16)],
                 dst_ref=target.at[lat, pl.ds(pl.multiple_of(here * 16, 16), 16)],
@@ -199,9 +200,6 @@
                 device_id={"space": peer},
                 device_id_type=MESH,
             ).start()
-            return carry
-
-        lax.fori_loop(0, SPACES - 1, one, 0)
         own = pl.ds(pl.multiple_of(here * 16, 16), 16)
         target[lat, own, :] = source[lat, own, :]
 
@@ -248,30 +246,30 @@
         most = pl.ds(0, count)
         pltpu.make_async_copy(coefs.at[0, most], coefs.at[0, most], sem).wait()
 
+    lane = lax.broadcasted_iota(jnp.int32, (64, 128), 1)
+    tail_lane = lane >= 96
+    flat[...] = jnp.zeros_like(flat)
     cols = cols_ref[...]
     for start in range(0, COLS, 128):
         hot[:, start : start + 128] = one_hot(cols, start, 128)
     load_x.wait()
     load_forward.wait()
+    for load in (load_coef, load_gain, load_inverse):
+        load.start()
     for lat in range(LDEV):
         weight = weight_ref[here * LDEV + lat]
         for k in range(2):
             part = jnp.dot(x_ref[lat], forward_ref[k], preferred_element_type=F32)
             zonal[k * CDEV : k * CDEV + CDEV, :] = (part * weight).astype(BF16)
         packed[...] = jnp.dot(zonal[...], hot[...], preferred_element_type=F32)
-        for pair in range(MAIN // 2):
-            main = packed[:, pair * 128 : pair * 128 + 128]
-            extra = jnp.zeros((32, 128), F32)
-            if pair < 3:
-                wide = packed[:, 1024 + pair * 128 : 1024 + pair * 128 + 128]
-                third = third_of(pair, (32, 128))
-                for th in range(3):
-                    extra = jnp.where(third == th, wide[th * 32 : th * 32 + 32], extra)
-            turned = jnp.concatenate([main, extra], axis=0).T
-            for half in range(2):
-                rows[lat, pl.ds(pair * 2 + half, 64, stride=16), :] = turned[
-                    half * 64 : half * 64 + 64
-                ]
+        for start in range(0, COLS, 128):
+            flat[start : start + 128, 0:96] = packed[:, start : start + 128].T
+        for row in range(MAIN):
+            line = flat[pl.ds(row, 64, stride=SLOTS), :]
+            if row < 6:
+                last = flat[pl.ds(MAIN + row // 3, 64, stride=SLOTS), :]
+                line = jnp.where(tail_lane, pltpu.roll(last, 96 - 32 * (row % 3), 1), line)
+            rows[lat, pl.ds(row, 64, stride=16), :] = line
         out_rows[lat] = rows[lat].astype(BF16)
         if lat == 0:
             pl.semaphore_wait(barrier, SPACES - 1 + CHANS - 1)
@@ -322,34 +320,24 @@
 
         lax.fori_loop(0, SLOTS, lay_out, 0)
 
-    wait_coef(3, coef_recv.at[0])
-    pltpu.make_async_remote_copy(
-        src_ref=coefs.at[core],
-        dst_ref=coefs.at[core],
-        send_sem=coef_send.at[1],
-        recv_sem=coef_recv.at[1],
-        device_id={"chan": sibling},
-        device_id_type=MESH,
-    ).start()
-
-    for lat in range(LDEV):
-        wait_space(out_rows, in_rows, recv_sem, 0, lat)
-        rows[lat] = in_rows[lat].astype(F32)
-    for row in range(MAIN):
-        stack = jnp.concatenate(
-            [rows[lat, pl.ds(row, 64, stride=16), :] for lat in range(LDEV)]
-            + [jnp.zeros((64, 128), F32)],
-            axis=0,
-        )
-        turned = stack.T.astype(BF16)
-        spread[row] = turned[0:96]
-        if row < 6:
-            at = 32 * (row % 3)
-            spread[MAIN + row // 3, at : at + 32, :] = turned[96:128]
+    for lats in ((0, 1), (2,)):
+        for lat in lats:
+            wait_space(out_rows, in_rows, recv_sem, 0, lat)
+            rows[lat] = in_rows[lat].astype(F32)
+        lanes = slice(lats[0] * 64, lats[0] * 64 + 128)
+        for row in range(MAIN):
+            stack = [rows[lat, pl.ds(row, 64, stride=16), :] for lat in lats]
+            if len(lats) == 1:
+                stack.append(jnp.zeros((64, 128), F32))
+            turned = jnp.concatenate(stack, axis=0).T.astype(BF16)
+            spread[row, :, lanes] = turned[0:96]
+            if row < 6:
+                at = 32 * (row % 3)
+                spread[MAIN + row // 3, at : at + 32, lanes] = turned[96:128]
     load_gain.wait()
 
     def filter_slots(step, carry):
-        slots = [step * 3 + i for i in range(3)]
+        slots = [step * 6 + i for i in range(6)]
         spectra = [
             lax.dot_general(
                 spread[slot], legendre[slot], (((1,), (1,)), ((), ())), preferred_element_type=F32
@@ -366,31 +354,31 @@
             made[slot] = jnp.dot(filtered, legendre[slot], preferred_element_type=F32)
         return carry
 
-    lax.fori_loop(0, SLOTS // 3, filter_slots, 0)
-    for row in range(MAIN):
-        extra = jnp.zeros((32, 256), F32)
-        if row < 6:
-            at = 32 * (row % 3)
-            extra = made[MAIN + row // 3, at : at + 32, :]
-        turned = jnp.concatenate([made[row], extra], axis=0).T
-        for lat in range(LDEV):
-            rows[lat, pl.ds(row, 64, stride=16), :] = turned[lat * 64 : lat * 64 + 64]
-    for lat in range(LDEV):
-        back_rows[lat] = rows[lat].astype(BF16)
-        send_space(back_rows, got_rows, 1, lat)
-
-    wait_coef(4, coef_recv.at[1])
-    for k in range(BASIS):
-        turned = jnp.concatenate(
-            [coefs[g % 2, g // 2, k] for g in range(CHANS)], axis=0
-        ).astype(F32).T
-        if k == 1:
-            bias_ref[...] = jnp.broadcast_to(
-                jnp.sum(turned, axis=1, keepdims=True), bias_ref.shape
-            )
-        else:
-            at = (k if k == 0 else k - 1) * 384
-            coef_ref[:, at : at + 384] = turned.astype(BF16)
+    lax.fori_loop(0, SLOTS // 6, filter_slots, 0)
+    for lats in ((0, 1), (2,)):
+        lanes = slice(lats[0] * 64, lats[0] * 64 + 128)
+        for row in range(MAIN):
+            extra = jnp.zeros((32, 128), F32)
+            if row < 6:
+                at = 32 * (row % 3)
+                extra = made[MAIN + row // 3, at : at + 32, lanes]
+            turned = jnp.concatenate([made[row, :, lanes], extra], axis=0).T
+            for i, lat in enumerate(lats):
+                rows[lat, pl.ds(row, 64, stride=16), :] = turned[i * 64 : i * 64 + 64]
+        for lat in lats:
+            back_rows[lat] = rows[lat].astype(BF16)
+            send_space(back_rows, got_rows, 1, lat)
+
+    wait_coef(3, coef_recv.at[0])
+    pltpu.make_async_remote_copy(
+        src_ref=coefs.at[core],
+        dst_ref=coefs.at[core],
+        send_sem=coef_send.at[1],
+        recv_sem=coef_recv.at[1],
+        device_id={"chan": sibling},
+        device_id_type=MESH,
+    ).start()
+
     load_inverse.wait()
 
     def mix(lat):
@@ -413,20 +401,39 @@
             )
         send_chan(mixed, final, 1, lat)
 
+    def prepare_coef():
+        wait_coef(4, coef_recv.at[1])
+        for k in range(BASIS):
+            turned = jnp.concatenate(
+                [coefs[g % 2, g // 2, k] for g in range(CHANS)], axis=0
+            ).astype(F32).T
+            if k == 1:
+                bias_ref[...] = jnp.broadcast_to(
+                    jnp.sum(turned, axis=1, keepdims=True), bias_ref.shape
+                )
+            else:
+                at = (k if k == 0 else k - 1) * 384
+                coef_ref[:, at : at + 384] = turned.astype(BF16)
+
     for lat in range(LDEV):
         wait_space(back_rows, got_rows, recv_sem, 1, lat)
         rows[lat] = got_rows[lat].astype(F32)
-        for pair in range(MAIN // 2):
-            turned = jnp.concatenate(
-                [rows[lat, pl.ds(pair * 2 + half, 64, stride=16), :] for half in range(2)], axis=0
-            ).T
-            gathered[:, pair * 128 : pair * 128 + 128] = turned[0:96].astype(BF16)
-            if pair < 3:
-                third = third_of(pair, (32, 128))
-                for th in range(3):
-                    gathered[
-                        th * 32 : th * 32 + 32, 1024 + pair * 128 : 1024 + pair * 128 + 128
-                    ] = jnp.where(third == th, turned[96:128], 0.0).astype(BF16)
+        for row in range(MAIN):
+            flat[pl.ds(row, 64, stride=SLOTS), :] = rows[lat, pl.ds(row, 64, stride=16), :]
+        for i in range(SLOTS - MAIN):
+            thirds = [
+                pltpu.roll(
+                    rows[lat, pl.ds(3 * i + th, 64, stride=16), :], (32 + 32 * th) % 128, 1
+                )
+                for th in range(3)
+            ]
+            flat[pl.ds(MAIN + i, 64, stride=SLOTS), :] = jnp.where(
+                lane < 32, thirds[0], jnp.where(lane < 64, thirds[1], thirds[2])
+            )
+        for start in range(0, COLS, 128):
+            gathered[:, start : start + 128] = (
+                flat[start : start + 128, :].T[0:96].astype(BF16)
+            )
         total = lax.dot_general(
             gathered[...], hot[...], (((1,), (1,)), ((), ())), preferred_element_type=F32
         )
@@ -451,19 +458,13 @@
                 for part, place in places(lat, block):
                     updated[lat, part, :, place * 128 : place * 128 + 128] = new
         send_chan(updated, whole, 0, lat)
-        if lat > 0:
+        if lat == 0:
+            prepare_coef()
+        else:
             mix(lat - 1)
     mix(LDEV - 1)
     for lat in range(LDEV):
         wait_chan(mixed, final, chan_recv, 1, lat)
-        for block in range(12):
-            part, place = places(lat, block)[0]
-            width = 128 if block < 11 else 32
-            out_ref[lat, :, block * 128 : block * 128 + width] = final[
-                lat, part, :, place * 128 : place * 128 + width
-            ]
-
-    for lat in range(LDEV):
         wait_space(out_rows, in_rows, send_sem, 0, lat)
         wait_space(back_rows, got_rows, send_sem, 1, lat)
         wait_chan(updated, whole, chan_send, 0, lat)
@@ -472,19 +473,25 @@
     wait_coef(4, coef_send.at[1])
 
 
+def unpack_kernel(final_ref, out_ref):
+    for lat in range(LDEV):
+        for block in range(12):
+            part, place = places(lat, block)[0]
+            width = 128 if block < 11 else 32
+            out_ref[lat, :, block * 128 : block * 128 + width] = final_ref[
+                lat, part, :, place * 128 : place * 128 + width
+            ]
+
+
 def shards(state_field, slot_wave, spectral_filter, kan_coef):
     forward, inverse, weights, xrow, first, steps = make_tables()
     x = jnp.transpose(state_field, (1, 0, 2))
-    slots = slot_wave.reshape(SPACES, SLOTS)
-    cols = jnp.concatenate(
-        [slots[:, :MAIN].T.reshape(-1)] + [slots[:, 16]] * 3 + [slots[:, 17]] * 3
-    )
-    cols = jnp.broadcast_to(cols[None, :], (8, COLS))
+    cols = slot_wave.reshape(1, COLS)
     message = pltpu.VMEM((LDEV, SPACES * 16, 128), BF16)
     part = pltpu.VMEM((LDEV, CHANS, CDEV, PART), BF16)
-    out = pl.pallas_call(
+    final = pl.pallas_call(
         block_kernel,
-        out_shape=jax.ShapeDtypeStruct((LDEV, CDEV, NLON), BF16),
+        out_shape=jax.ShapeDtypeStruct((LDEV, CHANS, CDEV, PART), BF16),
         in_specs=[HBM] * 5 + [SMEM] * 3 + [VMEM] * 3,
         out_specs=VMEM,
         scratch_shapes=[
@@ -503,6 +510,7 @@
             pltpu.VMEM((MPAD, COLS), BF16),
             pltpu.VMEM((96, MPAD), BF16),
             pltpu.VMEM((96, COLS), F32),
+            pltpu.VMEM((COLS, 128), F32),
             pltpu.VMEM((LDEV, SPACES * 16, 128), F32),
             message,
             message,
@@ -522,13 +530,19 @@
             part,
             part,
             part,
-            part,
         ],
         compiler_params=pltpu.CompilerParams(
             collective_id=0, has_side_effects=True, vmem_limit_bytes=60 * 1024 * 1024
         ),
         name="spectral_block",
     )(x, forward, inverse, spectral_filter, kan_coef, slot_wave, weights, steps, cols, xrow, first)
+    out = pl.pallas_call(
+        unpack_kernel,
+        out_shape=jax.ShapeDtypeStruct((LDEV, CDEV, NLON), BF16),
+        in_specs=[VMEM],
+        out_specs=VMEM,
+        name="unpack",
+    )(final)
     return jnp.transpose(out, (1, 0, 2))
 
 

time: 84.5 us -> 79.3 us (0.938)
  Pallas kernels: 80.6 us -> 77.8 us
  local copies, waits for them, and re-layouts: 3.66 us -> 1.29 us
    pallas_call x1 -> x2, Pallas kernels: 80.6 us -> 77.8 us  [the longest x1 75.9 us: shards(): pl.pallas_call(block_kernel, out_shape=jax.ShapeDtypeStruct((LDEV, CHANS,...]
    unnamed x1 -> x0, local copies, waits for them, and re-layouts: 1.8 us -> none
where the time goes in v4:
time: 79.3 us; the launch traced here: 79.1 us
  Pallas kernels  77.8 us (98%)
  local copies, waits for them, and re-layouts  1.29 us (2%)
    pallas_call x1, Pallas kernels, shards(): pl.pallas_call(block_kernel, out_shape=jax.ShapeDtypeStruct((LDEV, CHANS,...  75.9 us
    pallas_call x1, Pallas kernels, shards(): pl.pallas_call(unpack_kernel, out_shape=jax.ShapeDtypeStruct((LDEV, CDEV,...  1.87 us

profile of v4, /device:TPU:1, one launch (start us, length us, event | category | flops | bytes accessed | tf_op | source)
XLA Modules:
  0.0 79.1 jit_solution(2312151653512932382)
XLA Ops:
  0.0 1.3 %reshape.3.cols_ref = s32[1,1152]{1,0:T(1,128)} reshape(s32[1152]{0:T(1024)} %wave_ref.1) | data formatting | bytes 9216 | tf_op jit(solution)/shard_map/reshape | solution.py:489
  1.3 75.9 %spectral_block.1.final_ref = bf16[3,8,48,256]{3,2,1,0:T(8,128)(2,1)} custom-call(bf16[3,48,1440]{2,1,0:T(8,128)(2,1)} %bitcast.2, bf16[2,1440,768]{2,1,0:T(8,128)(2,1)} %constant.12.clone.forward_hbm, bf16[1536,1536]{1,0:T(8,128)(2,1)} %constant.13.clone.inverse_hbm, bf16[18,2,48,720]{3,2,1,0:T(8,128)(2,1)} %gain_hbm.1, bf16[6,48,384]{2,1,0:T(8,128)(2,1)} %coef_hbm.1, ...), custom_call_target="tpu_custom_call" | custom-call | tf_op jit(solution)/shard_map/spectral_block/pallas_call | solution.py:492
  77.2 1.9 %unpack.1 = bf16[3,48,1440]{2,1,0:T(8,128)(2,1)} custom-call(bf16[3,8,48,256]{3,2,1,0:T(8,128)(2,1)} %spectral_block.1.final_ref), custom_call_target="tpu_custom_call" | custom-call | tf_op jit(solution)/shard_map/unpack/pallas_call | solution.py:539

commit v5 on v4

--- a/solution.py
+++ b/solution.py
@@ -85,10 +85,6 @@
     ((k // 8, k % 8) for k in range(1, SPACES)),
     key=lambda step: -min(step[0], 8 - step[0]) - min(step[1], 8 - step[1]),
 )
-
-
-def far(i):
-    return 4 + ((i + 1) // 2) * (1 - 2 * (i % 2))
 
 
 def places(lat, block):
@@ -153,9 +149,6 @@
     chip, core = group // 2, group % 2
     sibling = chip * 2 + 1 - core
 
-    def space_peer(k):
-        return lax.rem(here_y + far(k // 8), 8) * 8 + lax.rem(here_z + far(k % 8), 8)
-
     loads = [
         pltpu.make_async_copy(source, target, load_sem.at[i])
         for i, (source, target) in enumerate(
@@ -174,20 +167,12 @@
 
     barrier = pltpu.get_barrier_semaphore()
 
-    def greet_space(k, carry):
-        pl.semaphore_signal(
-            barrier, inc=1, device_id={"space": space_peer(k)}, device_id_type=MESH
-        )
-        return carry
-
-    def greet_chan(k, carry):
-        pl.semaphore_signal(
-            barrier, inc=1, device_id={"chan": lax.rem(group + k, CHANS)}, device_id_type=MESH
-        )
-        return carry
-
-    lax.fori_loop(0, SPACES - 1, greet_space, 0)
-    lax.fori_loop(1, CHANS, greet_chan, 0)
+    for oy, oz in ORDER:
+        peer = lax.rem(here_y + oy, 8) * 8 + lax.rem(here_z + oz, 8)
+        pl.semaphore_signal(barrier, inc=1, device_id={"space": peer}, device_id_type=MESH)
+    for k in range(1, CHANS):
+        peer = lax.rem(group + k, CHANS)
+        pl.semaphore_signal(barrier, inc=1, device_id={"chan": peer}, device_id_type=MESH)
 
     def send_space(source, target, step, lat):
         for oy, oz in ORDER:
@@ -210,8 +195,8 @@
         ).wait()
 
     def send_chan(source, target, step, lat):
-        def one(k, carry):
-            peer = lax.rem(group + far(k), CHANS)
+        for offset in (4, 3, 5, 2, 6, 7, 1):
+            peer = lax.rem(group + offset, CHANS)
             pltpu.make_async_remote_copy(
                 src_ref=source.at[lat, peer],
                 dst_ref=target.at[lat, group],
@@ -220,9 +205,6 @@
                 device_id={"chan": peer},
                 device_id_type=MESH,
             ).start()
-            return carry
-
-        lax.fori_loop(0, CHANS - 1, one, 0)
         target[lat, group] = source[lat, group]
 
     def wait_chan(source, target, sem, step, lat):
@@ -337,7 +319,7 @@
     load_gain.wait()
 
     def filter_slots(step, carry):
-        slots = [step * 6 + i for i in range(6)]
+        slots = [step * 9 + i for i in range(9)]
         spectra = [
             lax.dot_general(
                 spread[slot], legendre[slot], (((1,), (1,)), ((), ())), preferred_element_type=F32
@@ -354,7 +336,7 @@
             made[slot] = jnp.dot(filtered, legendre[slot], preferred_element_type=F32)
         return carry
 
-    lax.fori_loop(0, SLOTS // 6, filter_slots, 0)
+    lax.fori_loop(0, SLOTS // 9, filter_slots, 0)
     for lats in ((0, 1), (2,)):
         lanes = slice(lats[0] * 64, lats[0] * 64 + 128)
         for row in range(MAIN):

time: 79.3 us -> 78.5 us (0.990)
  Pallas kernels: 77.8 us -> 76.9 us
    pallas_call x1, Pallas kernels: 75.9 us -> 75 us  [shards(): pl.pallas_call(block_kernel, out_shape=jax.ShapeDtypeStruct((LDEV, CHANS,...]
where the time goes in v5:
time: 78.5 us; the launch traced here: 78.2 us
  Pallas kernels  76.9 us (98%)
  local copies, waits for them, and re-layouts  1.29 us (2%)
    pallas_call x1, Pallas kernels, shards(): pl.pallas_call(block_kernel, out_shape=jax.ShapeDtypeStruct((LDEV, CHANS,...  75 us
    pallas_call x1, Pallas kernels, shards(): pl.pallas_call(unpack_kernel, out_shape=jax.ShapeDtypeStruct((LDEV, CDEV,...  1.87 us

profile of v5, /device:TPU:1, one launch (start us, length us, event | category | flops | bytes accessed | tf_op | source)
XLA Modules:
  0.0 78.2 jit_solution(15917930500218091401)
XLA Ops:
  0.0 1.3 %reshape.3.cols_ref = s32[1,1152]{1,0:T(1,128)} reshape(s32[1152]{0:T(1024)} %wave_ref.1) | data formatting | bytes 9216 | tf_op jit(solution)/shard_map/reshape | solution.py:471
  1.3 75.0 %spectral_block.1.final_ref = bf16[3,8,48,256]{3,2,1,0:T(8,128)(2,1)} custom-call(bf16[3,48,1440]{2,1,0:T(8,128)(2,1)} %bitcast.2, bf16[2,1440,768]{2,1,0:T(8,128)(2,1)} %constant.12.clone.forward_hbm, bf16[1536,1536]{1,0:T(8,128)(2,1)} %constant.13.clone.inverse_hbm, bf16[18,2,48,720]{3,2,1,0:T(8,128)(2,1)} %gain_hbm.1, bf16[6,48,384]{2,1,0:T(8,128)(2,1)} %coef_hbm.1, ...), custom_call_target="tpu_custom_call" | custom-call | tf_op jit(solution)/shard_map/spectral_block/pallas_call | solution.py:474
  76.3 1.9 %unpack.1 = bf16[3,48,1440]{2,1,0:T(8,128)(2,1)} custom-call(bf16[3,8,48,256]{3,2,1,0:T(8,128)(2,1)} %spectral_block.1.final_ref), custom_call_target="tpu_custom_call" | custom-call | tf_op jit(solution)/shard_map/unpack/pallas_call | solution.py:521

commit v6 on v5

--- a/solution.py
+++ b/solution.py
@@ -154,16 +154,18 @@
         for i, (source, target) in enumerate(
             (
                 (x_hbm, x_ref),
-                (forward_hbm, forward_ref),
+                (forward_hbm.at[0], forward_ref.at[0]),
+                (forward_hbm.at[1], forward_ref.at[1]),
                 (inverse_hbm, inverse_ref),
                 (gain_hbm, gain_ref),
                 (coef_hbm, coefs.at[core, chip]),
             )
         )
     ]
-    load_x, load_forward, load_inverse, load_gain, load_coef = loads
+    load_x, load_real, load_imag, load_inverse, load_gain, load_coef = loads
     load_x.start()
-    load_forward.start()
+    load_real.start()
+    load_imag.start()
 
     barrier = pltpu.get_barrier_semaphore()
 
@@ -235,14 +237,16 @@
     for start in range(0, COLS, 128):
         hot[:, start : start + 128] = one_hot(cols, start, 128)
     load_x.wait()
-    load_forward.wait()
-    for load in (load_coef, load_gain, load_inverse):
-        load.start()
     for lat in range(LDEV):
         weight = weight_ref[here * LDEV + lat]
         for k in range(2):
+            if lat == 0:
+                (load_real, load_imag)[k].wait()
             part = jnp.dot(x_ref[lat], forward_ref[k], preferred_element_type=F32)
             zonal[k * CDEV : k * CDEV + CDEV, :] = (part * weight).astype(BF16)
+        if lat == 0:
+            for load in (load_coef, load_gain, load_inverse):
+                load.start()
         packed[...] = jnp.dot(zonal[...], hot[...], preferred_element_type=F32)
         for start in range(0, COLS, 128):
             flat[start : start + 128, 0:96] = packed[:, start : start + 128].T
@@ -482,7 +486,7 @@
             pltpu.VMEM((2 * MPAD, NPAD), BF16),
             pltpu.VMEM((SLOTS, 2, CDEV, LMAX), BF16),
             pltpu.VMEM((2, CHANS // 2, BASIS, CDEV, 384), BF16),
-            pltpu.SemaphoreType.DMA((5,)),
+            pltpu.SemaphoreType.DMA((6,)),
             pltpu.SemaphoreType.DMA((2, LDEV)),
             pltpu.SemaphoreType.DMA((2, LDEV)),
             pltpu.SemaphoreType.DMA((2, LDEV)),

time: 78.5 us -> 78.9 us (level)
  no operation moved by 1% of the time
where the time goes in v6:
time: 78.9 us; the launch traced here: 78.7 us
  Pallas kernels  77.4 us (98%)
  local copies, waits for them, and re-layouts  1.29 us (2%)
    pallas_call x1, Pallas kernels, shards(): pl.pallas_call(block_kernel, out_shape=jax.ShapeDtypeStruct((LDEV, CHANS,...  75.5 us
    pallas_call x1, Pallas kernels, shards(): pl.pallas_call(unpack_kernel, out_shape=jax.ShapeDtypeStruct((LDEV, CDEV,...  1.87 us

profile of v6, /device:TPU:1, one launch (start us, length us, event | category | flops | bytes accessed | tf_op | source)
XLA Modules:
  0.0 78.7 jit_solution(14313156748290518767)
XLA Ops:
  0.0 1.3 %reshape.3.cols_ref = s32[1,1152]{1,0:T(1,128)} reshape(s32[1152]{0:T(1024)} %wave_ref.1) | data formatting | bytes 9216 | tf_op jit(solution)/shard_map/reshape | solution.py:475
  1.3 75.5 %spectral_block.1.final_ref = bf16[3,8,48,256]{3,2,1,0:T(8,128)(2,1)} custom-call(bf16[3,48,1440]{2,1,0:T(8,128)(2,1)} %bitcast.2, bf16[2,1440,768]{2,1,0:T(8,128)(2,1)} %constant.12.clone.forward_hbm, bf16[1536,1536]{1,0:T(8,128)(2,1)} %constant.13.clone.inverse_hbm, bf16[18,2,48,720]{3,2,1,0:T(8,128)(2,1)} %gain_hbm.1, bf16[6,48,384]{2,1,0:T(8,128)(2,1)} %coef_hbm.1, ...), custom_call_target="tpu_custom_call" | custom-call | tf_op jit(solution)/shard_map/spectral_block/pallas_call | solution.py:478
  76.8 1.9 %unpack.1 = bf16[3,48,1440]{2,1,0:T(8,128)(2,1)} custom-call(bf16[3,8,48,256]{3,2,1,0:T(8,128)(2,1)} %spectral_block.1.final_ref), custom_call_target="tpu_custom_call" | custom-call | tf_op jit(solution)/shard_map/unpack/pallas_call | solution.py:525
